TPU v7x, 512 devices: a whole 4x4x16 slice. The times are simulated.
512 devices in a mesh: wide: 32 (over z, core), sub: 16 (over x, y).
Axes of the slice: x: 4, y: 4, z: 16, core: 2. Of those that a mesh axis runs over, the one named last changes fastest.
Arguments:
- passages: bfloat16 [256, 1024], P('sub'), may hold values from -6 to 6
- enc_weight: bfloat16 [1024, 262144], P(None, ('wide', 'sub')), may hold values from -0.1875 to 0.1875
- enc_bias: float32 [262144], P(('wide', 'sub')), may hold values from -4 to 4
- dec_weight: bfloat16 [262144, 1024], P(('wide', 'sub')), may hold values from -0.0234375 to 0.0234375
- dec_bias: float32 [1024], replicated, may hold values from -4 to 4
- active: int32 [256, 262144], P(None, ('wide', 'sub')), may hold values 0 or 1
Outputs:
- grad_enc: bfloat16 [1024, 262144], P(None, ('wide', 'sub'))
- grad_enc_bias: float32 [262144], P(('wide', 'sub'))
- grad_dec: bfloat16 [262144, 1024], P(('wide', 'sub'))
- grad_dec_bias: float32 [1024], replicated
- grad_input: float32 [256, 1024], P('sub')
All inputs are finite; a program needn't handle non-finite values. No bound on the sum of `active` on one device may be relied on, other than what follows from the above.
Results may differ from a plain program's by a relative error of at most 0.014.
Values may be sent and summed in bfloat16 or wider, within the bound.
A program may use at most 64 MiB of HBM per device.

v0:
```python
import jax
import jax.numpy as jnp
from jax import lax
from jax.sharding import Mesh
from jax.sharding import PartitionSpec as P

SUB = ("sub_0", "sub_1")
WIDE_SUB = ("wide_0", "wide_1", "sub_0", "sub_1")
WIDE = ("wide_0", "wide_1")


def in_order(blocks, dim):
    dims = list(blocks.shape[1:])
    dims[dim] *= blocks.shape[0]
    return jnp.moveaxis(blocks, 0, dim).reshape(dims)


def from_everyone(array, axis):
    copies = jnp.broadcast_to(array, (lax.axis_size(axis), *array.shape))
    return lax.all_to_all(copies, axis, split_axis=0, concat_axis=0, tiled=True)


def gathered_copies(array, axis, dim):
    return in_order(from_everyone(array, axis), dim)


def filled_up(lines, count):
    spare = -lines.shape[0] % count
    if not spare:
        return lines
    return jnp.concatenate([lines, jnp.zeros((spare, *lines.shape[1:]), lines.dtype)])


def gather_axes(array, axes, dim):
    far, near = axes
    blocks = from_everyone(from_everyone(array, far), near)
    return in_order(blocks.swapaxes(0, 1).reshape(-1, *array.shape), dim)


def split_up(array, dim, count):
    dims = array.shape
    blocks = array.reshape(*dims[:dim], count, dims[dim] // count, *dims[dim + 1 :])
    return jnp.moveaxis(blocks, dim, 0)


def sent_and_summed(array, axis, dim):
    count = lax.axis_size(axis)
    blocks = lax.all_to_all(split_up(array, dim, count), axis, 0, 0, tiled=True)
    return jnp.sum(blocks, axis=0)


def sum_in_two_steps(array, axes, dim):
    far, near = axes
    own = sent_and_summed(split_up(array, dim, lax.axis_size(far)), near, dim + 1)
    return jnp.sum(lax.all_to_all(own, far, 0, 0, tiled=True), axis=0)


def sum_by_parts(array, axes):
    lines = array.reshape(-1)
    padded = filled_up(lines, lax.axis_size(axes[0]) * lax.axis_size(axes[1]))
    whole = gather_axes(sum_in_two_steps(padded, axes, 0), axes, 0)
    return lax.slice_in_dim(whole, 0, len(lines)).reshape(array.shape)


def summed_on_arrival(array, axis, dim):
    blocks = split_up(array, dim, lax.axis_size(axis))
    arrived = lax.all_to_all(blocks, axis, split_axis=0, concat_axis=0, tiled=True)
    return arrived.astype(jnp.float32).sum(axis=0)


def sum_by_parts_2(array, axes):
    lines = array.reshape(-1)
    own = summed_on_arrival(filled_up(lines, lax.axis_size(axes)), axes, 0)
    whole = gathered_copies(own.astype(jnp.bfloat16), axes, 0)
    return whole[: len(lines)].reshape(array.shape).astype(jnp.float32)


def per_device(passages, enc_weight, enc_bias, dec_weight, dec_bias, active):
    owned = passages.shape[0]
    gate = active.astype(jnp.float32)
    every = gathered_copies(passages, SUB, 0)
    offset = lax.axis_index(SUB) * owned
    pre = jnp.dot(every, enc_weight, preferred_element_type=jnp.float32) + enc_bias
    codes = (gate * pre).astype(jnp.bfloat16)
    whole = sum_by_parts(
        jnp.dot(codes, dec_weight, preferred_element_type=jnp.float32),
        (("wide_0", "wide_1"), ("sub_0", "sub_1")),
    )
    resid = (whole + dec_bias - every.astype(jnp.float32)).astype(jnp.bfloat16)
    own_resid = lax.dynamic_slice_in_dim(resid, offset, owned, 0)
    grad_dec = lax.dot_general(
        codes, resid, (((0,), (0,)), ((), ())), preferred_element_type=jnp.float32
    ).astype(jnp.bfloat16)
    grad_dec_bias = jnp.sum(resid.astype(jnp.float32), axis=0)
    back = lax.dot_general(
        resid, dec_weight, (((1,), (1,)), ((), ())), preferred_element_type=jnp.float32
    )
    dpre = (gate * back).astype(jnp.bfloat16)
    grad_enc = lax.dot_general(
        every, dpre, (((0,), (0,)), ((), ())), preferred_element_type=jnp.float32
    ).astype(jnp.bfloat16)
    grad_enc_bias = jnp.sum(dpre.astype(jnp.float32), axis=0)
    summed = summed_on_arrival(
        lax.dot_general(
            dpre, enc_weight, (((1,), (1,)), ((), ())), preferred_element_type=jnp.float32
        ).astype(jnp.bfloat16),
        SUB,
        0,
    )
    summed = sum_by_parts_2(summed.astype(jnp.bfloat16), WIDE)
    grad_input = summed - own_resid.astype(jnp.float32)
    return (grad_enc, grad_enc_bias, grad_dec, grad_dec_bias, grad_input)


def solution(mesh):
    split = Mesh(mesh.devices.reshape(16, 2, 4, 4), ("wide_0", "wide_1", "sub_0", "sub_1"))
    placed = (
        P(SUB, None),
        P(None, WIDE_SUB),
        P(WIDE_SUB),
        P(WIDE_SUB, None),
        P(),
        P(None, WIDE_SUB),
    )
    return jax.shard_map(
        per_device,
        mesh=split,
        in_specs=placed,
        out_specs=(P(None, WIDE_SUB), P(WIDE_SUB), P(WIDE_SUB, None), P(), P(SUB, None)),
        check_vma=False,
    )
```

profile of v0, /device:TPU:1, one launch (start us, length us, event | category | flops | bytes accessed | tf_op | source)
XLA Modules:
  0.0 174.5 jit_solution(10044477755818114364)
XLA Ops:
  0.7 1.0 broadcast_in_dim.14
  1.6 16.6 %all_to_all.54 = bf16[16,16,1024]{2,1,0:T(8,128)(2,1)S(1)} all-to-all(bf16[16,16,1024]{2,1,0:T(8,128)(2,1)S(1)} %broadcast_in_dim.14), channel_id=1, replica_groups=mesh['wide_0'=16,'wide_1'=2,'sub_0'=4,'sub_1'=4] {'sub_0','sub_1'}, dimensions={0} | all-to-all | bytes 1048576 | tf_op jit(solution)/shard_map/all_to_all | solution.py:20
  18.7 1.4 fusion.4
  20.1 2.4 %reshape_reshape_reshape.6 = f32[32,16,512]{2,1,0:T(8,128)} reshape(f32[256,1024]{1,0:T(8,128)} %fusion.4) | data formatting | bytes 2097152 | tf_op jit(solution)/shard_map/reshape;reshape;reshape | solution.py:42
  22.5 1.8 %copy.21 = f32[32,16,512]{2,0,1:T(8,128)S(1)} copy(f32[32,16,512]{2,1,0:T(8,128)} %reshape_reshape_reshape.6) | data formatting | bytes 2097152 | tf_op jit(solution)/shard_map/reshape;reshape;reshape | solution.py:42
  24.3 16.6 %all_to_all.55 = f32[16,32,512]{2,1,0:T(8,128)} all-to-all(f32[16,32,512]{2,1,0:T(8,128)S(1)} %bitcast.27), channel_id=1, replica_groups=mesh['wide_0'=16,'wide_1'=2,'sub_0'=4,'sub_1'=4] {'sub_0','sub_1'}, dimensions={0} | all-to-all | bytes 2097152 | tf_op jit(solution)/shard_map/all_to_all | solution.py:48
  40.9 1.3 reduce_sum.60
  42.3 34.1 %all_to_all.56 = f32[32,1,512]{2,1,0:T(1,128)S(1)} all-to-all(f32[32,1,512]{2,1,0:T(1,128)S(1)} %all_to_all.36), channel_id=1, replica_groups=mesh['wide_0'=16,'wide_1'=2,'sub_0'=4,'sub_1'=4] {'wide_0','wide_1'}, dimensions={0} | all-to-all | bytes 131072 | tf_op jit(solution)/shard_map/all_to_all | solution.py:55
  76.4 17.3 %all_to_all.57 = f32[32,1,512]{2,1,0:T(1,128)S(1)} all-to-all(f32[32,1,512]{2,1,0:T(1,128)S(1)} %broadcast_in_dim.15), channel_id=1, replica_groups=mesh['wide_0'=16,'wide_1'=2,'sub_0'=4,'sub_1'=4] {'wide_0','wide_1'}, dimensions={0} | all-to-all | bytes 131072 | tf_op jit(solution)/shard_map/all_to_all | solution.py:20
  93.8 18.0 %all_to_all.58 = f32[16,32,512]{2,1,0:T(8,128)S(1)} all-to-all(f32[16,32,512]{2,1,0:T(8,128)S(1)} %broadcast_in_dim.16), channel_id=1, replica_groups=mesh['wide_0'=16,'wide_1'=2,'sub_0'=4,'sub_1'=4] {'sub_0','sub_1'}, dimensions={0} | all-to-all | bytes 2097152 | tf_op jit(solution)/shard_map/all_to_all | solution.py:20
  111.8 1.6 copy.15
  113.4 2.5 %reshape_reshape_reshape.7 = f32[256,1024]{1,0:T(8,128)} reshape(f32[32,16,512]{2,1,0:T(8,128)} %copy.15) | data formatting | bytes 2097152 | tf_op jit(solution)/shard_map/reshape;reshape;reshape | solution.py:62
  115.9 2.1 %convert_reduce_fusion = (f32[1024]{0:T(1024)}, bf16[256,1024]{1,0:T(8,128)(2,1)S(1)}) fusion(bf16[16,16,1024]{2,1,0:T(8,128)(2,1)S(1)} %all_to_all.54, f32[256,1024]{1,0:T(8,128)} %reshape_reshape_reshape.7, f32[1024]{0:T(1024)S(1)} %copy-done.5), kind=kLoop, calls=%fused_computation.10 | loop fusion | flops 1571840 | bytes 2105344 | tf_op jit(solution)/shard_map/reduce_sum | solution.py:94
  118.0 1.1 convert_reduce_fusion.1
  119.1 1.3 convolution_convert_fusion.2
  120.4 3.6 %all-to-all-start.5 = ((bf16[16,16,1024]{2,1,0:T(8,128)(2,1)}), bf16[16,16,1024]{2,1,0:T(8,128)(2,1)S(1)}, u32[]{:S(2)}, u32[]{:S(2)}) async-start(bf16[16,16,1024]{2,1,0:T(8,128)(2,1)} %bitcast.29), calls=%async_computation.5 | async-start | bytes 1048576 | tf_op jit(solution)/shard_map/all_to_all | solution.py:67
  124.0 8.9 %all-to-all-done.5 = bf16[16,16,1024]{2,1,0:T(8,128)(2,1)S(1)} async-done(((bf16[16,16,1024]{2,1,0:T(8,128)(2,1)}), bf16[16,16,1024]{2,1,0:T(8,128)(2,1)S(1)}, u32[]{:S(2)}, u32[]{:S(2)}) %all-to-all-start.5) | async-done | bytes 524320 | tf_op jit(solution)/shard_map/all_to_all | solution.py:67
  135.0 8.0 %all-to-all-start.6 = ((bf16[32,2,256]{2,1,0:T(2,128)(2,1)}), bf16[32,2,256]{2,1,0:T(2,128)(2,1)S(1)}, u32[]{:S(2)}, u32[]{:S(2)}) async-start(bf16[32,2,256]{2,1,0:T(2,128)(2,1)} %reshape.38), calls=%async_computation.6 | async-start | bytes 65536 | tf_op jit(solution)/shard_map/all_to_all | solution.py:67
  142.9 1.4 fusion
  144.3 10.7 %all-to-all-done.6 = bf16[32,2,256]{2,1,0:T(2,128)(2,1)S(1)} async-done(((bf16[32,2,256]{2,1,0:T(2,128)(2,1)}), bf16[32,2,256]{2,1,0:T(2,128)(2,1)S(1)}, u32[]{:S(2)}, u32[]{:S(2)}) %all-to-all-start.6) | async-done | bytes 32800 | tf_op jit(solution)/shard_map/all_to_all | solution.py:67
  156.7 4.6 %all-to-all-start.7 = ((bf16[32,2,256]{2,1,0:T(2,128)(2,1)}), bf16[32,2,256]{2,1,0:T(2,128)(2,1)S(1)}, u32[]{:S(2)}, u32[]{:S(2)}) async-start(bf16[32,2,256]{2,1,0:T(2,128)(2,1)} %reshape.40), calls=%async_computation.7 | async-start | bytes 65536 | tf_op jit(solution)/shard_map/all_to_all | solution.py:20
  161.3 1.4 convolution_convert_fusion
  162.7 1.3 copy.17
  164.0 9.5 %all-to-all-done.7 = bf16[32,2,256]{2,1,0:T(2,128)(2,1)S(1)} async-done(((bf16[32,2,256]{2,1,0:T(2,128)(2,1)}), bf16[32,2,256]{2,1,0:T(2,128)(2,1)S(1)}, u32[]{:S(2)}, u32[]{:S(2)}) %all-to-all-start.7) | async-done | bytes 32800 | tf_op jit(solution)/shard_map/all_to_all | solution.py:20
  (34 shorter events, 5.3 us)
Async XLA Ops:
  0.6 18.1 %copy-start = (bf16[512,1024]{1,0:T(8,128)(2,1)S(1)}, bf16[512,1024]{1,0:T(8,128)(2,1)}, u32[]{:S(2)}) copy-start(bf16[512,1024]{1,0:T(8,128)(2,1)} %param.9) | copy-start | bytes 3145732
  0.6 17.6 %copy-start.3 = (s32[256,512]{1,0:T(8,128)S(1)}, s32[256,512]{1,0:T(8,128)}, u32[]{:S(2)}) copy-start(s32[256,512]{1,0:T(8,128)} %param.11) | copy-start | bytes 1572868
  0.7 17.6 %copy-start.1 = (bf16[1024,512]{1,0:T(8,128)(2,1)S(1)}, bf16[1024,512]{1,0:T(8,128)(2,1)}, u32[]{:S(2)}) copy-start(bf16[1024,512]{1,0:T(8,128)(2,1)} %param.7) | copy-start | bytes 3145732
  0.7 17.6 %copy-start.6 = (f32[512]{0:T(512)S(1)}, f32[512]{0:T(512)}, u32[]{:S(2)}) copy-start(f32[512]{0:T(512)} %param.8) | copy-start | bytes 6148
  113.4 2.5 %copy-start.5 = (f32[1024]{0:T(1024)S(1)}, f32[1024]{0:T(1024)}, u32[]{:S(2)}) copy-start(f32[1024]{0:T(1024)} %param.10) | copy-start | bytes 12292
  115.9 2.1 %copy-start.4 = (s32[256,512]{1,0:T(8,128)S(1)}, s32[256,512]{1,0:T(8,128)}, u32[]{:S(2)}) copy-start(s32[256,512]{1,0:T(8,128)} %param.11) | copy-start | bytes 1572868
  119.1 1.3 copy-start.2
  120.4 12.5 %all-to-all-start.5 = ((bf16[16,16,1024]{2,1,0:T(8,128)(2,1)}), bf16[16,16,1024]{2,1,0:T(8,128)(2,1)S(1)}, u32[]{:S(2)}, u32[]{:S(2)}) async-start(bf16[16,16,1024]{2,1,0:T(8,128)(2,1)} %bitcast.29), calls=%async_computation.5 | async-start | bytes 1048576 | tf_op jit(solution)/shard_map/all_to_all | solution.py:67
  135.0 20.1 %all-to-all-start.6 = ((bf16[32,2,256]{2,1,0:T(2,128)(2,1)}), bf16[32,2,256]{2,1,0:T(2,128)(2,1)S(1)}, u32[]{:S(2)}, u32[]{:S(2)}) async-start(bf16[32,2,256]{2,1,0:T(2,128)(2,1)} %reshape.38), calls=%async_computation.6 | async-start | bytes 65536 | tf_op jit(solution)/shard_map/all_to_all | solution.py:67
  156.7 16.9 %all-to-all-start.7 = ((bf16[32,2,256]{2,1,0:T(2,128)(2,1)}), bf16[32,2,256]{2,1,0:T(2,128)(2,1)S(1)}, u32[]{:S(2)}, u32[]{:S(2)}) async-start(bf16[32,2,256]{2,1,0:T(2,128)(2,1)} %reshape.40), calls=%async_computation.7 | async-start | bytes 65536 | tf_op jit(solution)/shard_map/all_to_all | solution.py:20
where the time goes:
time: 175 us; the launch traced here: 174 us
  blocking collectives  103 us (59%)
  waiting for transfers between devices  29.1 us (17%)
  starting transfers between devices  16.2 us (9%)
  local copies, waits for them, and re-layouts  12.7 us (7%)
  matrix products  7.01 us (4%)
  other arithmetic  6.09 us (3%)
    all_to_all x3, blocking collectives, from_everyone(): return lax.all_to_all(copies, axis, split_axis=0, concat_axis=0, tiled=True)  51.8 us
    all_to_all x1, blocking collectives, sum_in_two_steps(): return jnp.sum(lax.all_to_all(own, far, 0, 0, tiled=True), axis=0)  34.1 us
    all_to_all x2, waiting for transfers between devices, summed_on_arrival(): lax.all_to_all(blocks, axis, split_axis=0, concat_axis=0, tiled=True)  19.6 us
    all_to_all x1, blocking collectives, sent_and_summed(): blocks = lax.all_to_all(split_up(array, dim, count), axis, 0, 0, tiled=True)  16.6 us
    all_to_all x2, starting transfers between devices, summed_on_arrival(): lax.all_to_all(blocks, axis, split_axis=0, concat_axis=0, tiled=True)  11.5 us
    all_to_all x1, waiting for transfers between devices, from_everyone(): return lax.all_to_all(copies, axis, split_axis=0, concat_axis=0, tiled=True)  9.53 us
    all_to_all x1, starting transfers between devices, from_everyone(): return lax.all_to_all(copies, axis, split_axis=0, concat_axis=0, tiled=True)  4.63 us
    another operation x2, local copies, waits for them, and re-layouts, split_up(): array.reshape(*dims[:dim], count, dims[dim] // count, *dims[dim + 1:])  4.19 us
  transfers between devices with their start and end apart: 3, of which 3 were waited for; matrix products, arithmetic and copies ran while one was open for 2% of the time, Pallas kernels for 0%

commit v1 on v0

v1 whole, which is shorter than its diff:
```python
import functools

import jax
import jax.numpy as jnp
from jax import lax
from jax.experimental import pallas as pl
from jax.experimental.pallas import tpu as pltpu
from jax.sharding import PartitionSpec as P

MESH = pl.DeviceIdType.MESH
BF16 = jnp.bfloat16
F32 = jnp.float32
ROWS, D, LAT = 256, 1024, 512
OWN, HALF, QUARTER = 16, 512, 256
SIDE, DEPTH = 4, 16


def ring(d, n):
    return min(d, n - d)


def dot_nt(a, b):
    return lax.dot_general(a, b, (((1,), (1,)), ((), ())), preferred_element_type=F32)


def dot_nn(a, b):
    return jnp.dot(a, b, preferred_element_type=F32)


def kernel(
    pas_in, enc_in, eb, dec_in, db, act_in,
    genc_out, geb_out, gdec_out, gdb_out, gin_out,
    enc, dec, act, every, every_t, pre, codes, codes_t, resid, dpre,
    swap_out, swap_in, parts, rows_in, rows_z, gdec, genc, final,
    load_sem, store_sem, send_sem, recv_sem, swap_send, swap_recv,
):
    wide, sub = lax.axis_index("wide"), lax.axis_index("sub")
    z, c = wide // 2, wide % 2
    x, y = sub // SIDE, sub % SIDE
    zp = z % 2
    zn = z + 1 - 2 * zp
    oc = 1 - c
    mine = pl.ds(pl.multiple_of(sub * OWN, OWN), OWN)

    sub_offsets = sorted(
        ((dx, dy) for dx in range(SIDE) for dy in range(SIDE)),
        key=lambda o: -ring(o[0], SIDE) - ring(o[1], SIDE),
    )
    subs = [((x + dx) % SIDE) * SIDE + (y + dy) % SIDE for dx, dy in sub_offsets]
    others = subs[:-1]
    sibling = (z * 2 + oc, sub)
    z_peers = [
        (((z + d) % DEPTH) * 2 + c, sub)
        for d in sorted(range(1, DEPTH), key=lambda d: -ring(d, DEPTH))
    ]

    loads = [
        pltpu.make_async_copy(
            pas_in.at[:, pl.ds(pl.multiple_of(c * HALF, HALF), HALF)],
            every.at[c, mine],
            load_sem.at[0],
        ),
        pltpu.make_async_copy(enc_in, enc, load_sem.at[1]),
        pltpu.make_async_copy(act_in, act, load_sem.at[2]),
        pltpu.make_async_copy(dec_in, dec, load_sem.at[3]),
    ]
    for load in loads:
        load.start()

    barrier = pltpu.get_barrier_semaphore()
    greeted = [(wide, s) for s in others] + [(zn * 2 + c, s) for s in others]
    greeted += z_peers + [sibling]
    for peer in greeted:
        pl.semaphore_signal(barrier, inc=1, device_id=peer, device_id_type=MESH)
    loads[0].wait()
    pl.semaphore_wait(barrier, len(greeted))

    def send(src, dst, k, peer):
        pltpu.make_async_remote_copy(
            src_ref=src, dst_ref=dst, send_sem=send_sem.at[k], recv_sem=recv_sem.at[k],
            device_id=peer, device_id_type=MESH,
        ).start()

    def arrived(ref, k):
        pltpu.make_async_copy(ref, ref, recv_sem.at[k]).wait()

    def sent(ref, k):
        pltpu.make_async_copy(ref, ref, send_sem.at[k]).wait()

    def swap(src, dst, k):
        copy = pltpu.make_async_remote_copy(
            src_ref=src, dst_ref=dst, send_sem=swap_send.at[k], recv_sem=swap_recv.at[k],
            device_id=sibling, device_id_type=MESH,
        )
        copy.start()
        return copy

    def gather(array, k, swap_k):
        for s in others:
            send(array.at[c, mine], array.at[c, mine], k, (wide, s))
        rest = array.at[c, pl.ds(0, ROWS - OWN)]
        arrived(rest, k)
        return swap(array.at[c], array.at[c], swap_k), rest

    def half(h):
        return pl.ds(pl.multiple_of(h * HALF, HALF), HALF)

    def quarter(q):
        return pl.ds(pl.multiple_of(q * QUARTER, QUARTER), QUARTER)

    def reduce_out(i, part):
        swaps = []
        for t in range(2):
            zq = zp if t else 1 - zp
            swap_out[i, t] = part(oc * 2 + zq).astype(BF16)
            swaps.append(swap(swap_out.at[i, t], swap_in.at[i, t], 2 + 2 * i + t))
        slot = zp * 16 + sub
        k = 2 + 2 * i
        for t in range(2):
            zq = zp if t else 1 - zp
            own = part(c * 2 + zq)
            swaps[t].wait_recv()
            parts[i, t] = (own + swap_in[i, t].astype(F32)).astype(BF16)
            for s in others if t else subs:
                rows = pl.ds(pl.multiple_of(s * OWN, OWN), OWN)
                peer = (wide if t else zn * 2 + c, s)
                send(parts.at[i, t, rows], rows_in.at[i, slot], k, peer)
        rows_in[i, slot] = parts[i, 1, mine]
        return swaps

    def pieces_along_z(i):
        k = 2 + 2 * i
        arrived(rows_in.at[i, pl.ds(0, 31)], k)
        total = rows_in[i, 0].astype(F32)
        for n in range(1, 32):
            total = total + rows_in[i, n].astype(F32)
        rows_z[i, z] = total.astype(BF16)
        for peer in z_peers:
            send(rows_z.at[i, z], rows_z.at[i, z], k + 1, peer)

    def sum_along_z(i, zq):
        total = rows_z[i, zq].astype(F32)
        for n in range(1, DEPTH // 2):
            total = total + rows_z[i, 2 * n + zq].astype(F32)
        return total

    def reduce_sent(i, swaps):
        for copy in swaps:
            copy.wait_send()
        sent(rows_in.at[i, pl.ds(0, 31)], 2 + 2 * i)
        sent(rows_z.at[i, pl.ds(0, 15)], 3 + 2 * i)

    passages_swap, passages_rest = gather(every, 0, 0)
    loads[1].wait()
    pre[...] = dot_nn(every[c], enc[half(c), :])
    loads[2].wait()
    loads[3].wait()
    passages_swap.wait_recv()
    both = pre[...] + dot_nn(every[oc], enc[half(oc), :]) + eb[...]
    codes[...] = (act[...].astype(F32) * both).astype(BF16)

    swaps_0 = reduce_out(0, lambda q: dot_nn(codes[...], dec[:, quarter(q)]))
    codes_t[...] = codes[...].T
    pieces_along_z(0)
    every_t[0] = every[0].T
    every_t[1] = every[1].T
    arrived(rows_z.at[0, pl.ds(0, 15)], 3)
    for zq in range(2):
        recon = sum_along_z(0, zq) + db[:, quarter(c * 2 + zq)]
        columns = pl.ds(zq * QUARTER, QUARTER)
        resid[c, mine, columns] = (recon - every[c, mine, columns].astype(F32)).astype(BF16)
    resid_swap, resid_rest = gather(resid, 1, 1)
    pre[...] = dot_nt(resid[c], dec[:, half(c)])
    resid_swap.wait_recv()
    back = pre[...] + dot_nt(resid[oc], dec[:, half(oc)])
    dpre[...] = (act[...].astype(F32) * back).astype(BF16)

    swaps_1 = reduce_out(1, lambda q: dot_nt(dpre[...], enc[quarter(q), :]))
    stores = []
    for h in range(2):
        gdec[:, pl.ds(h * HALF, HALF)] = dot_nn(codes_t[...], resid[h]).astype(BF16)
        gdb_out[:, pl.ds(h * HALF, HALF)] = jnp.sum(resid[h].astype(F32), axis=0, keepdims=True)
    stores.append(pltpu.make_async_copy(gdec, gdec_out, store_sem.at[0]))
    stores[0].start()
    for h in range(2):
        genc[pl.ds(h * HALF, HALF), :] = dot_nn(every_t[h], dpre[...]).astype(BF16)
    stores.append(pltpu.make_async_copy(genc, genc_out, store_sem.at[1]))
    stores[1].start()
    geb_out[...] = jnp.sum(dpre[...].astype(F32), axis=0, keepdims=True)
    pieces_along_z(1)
    passages_swap.wait_send()
    resid_swap.wait_send()
    sent(passages_rest, 0)
    sent(resid_rest, 1)
    reduce_sent(0, swaps_0)
    arrived(rows_z.at[1, pl.ds(0, 15)], 5)
    for zq in range(2):
        final[c, :, pl.ds(zq * QUARTER, QUARTER)] = sum_along_z(1, zq)
    final_swap = swap(final.at[c], final.at[c], 6)
    reduce_sent(1, swaps_1)
    for store in stores:
        store.wait()
    final_swap.wait()
    for h in range(2):
        gin_out[:, pl.ds(h * HALF, HALF)] = final[h] - resid[h, mine].astype(F32)


def per_device(passages, enc_weight, enc_bias, dec_weight, dec_bias, active):
    anywhere = pl.BlockSpec(memory_space=pl.ANY)
    vmem = pl.BlockSpec(memory_space=pltpu.VMEM)
    genc, geb, gdec, gdb, gin = pl.pallas_call(
        kernel,
        out_shape=(
            jax.ShapeDtypeStruct((D, LAT), BF16),
            jax.ShapeDtypeStruct((1, LAT), F32),
            jax.ShapeDtypeStruct((LAT, D), BF16),
            jax.ShapeDtypeStruct((1, D), F32),
            jax.ShapeDtypeStruct((OWN, D), F32),
        ),
        in_specs=[anywhere, anywhere, vmem, anywhere, vmem, anywhere],
        out_specs=(anywhere, vmem, anywhere, vmem, vmem),
        scratch_shapes=[
            pltpu.VMEM((D, LAT), BF16),
            pltpu.VMEM((LAT, D), BF16),
            pltpu.VMEM((ROWS, LAT), jnp.int32),
            pltpu.VMEM((2, ROWS, HALF), BF16),
            pltpu.VMEM((2, HALF, ROWS), BF16),
            pltpu.VMEM((ROWS, LAT), F32),
            pltpu.VMEM((ROWS, LAT), BF16),
            pltpu.VMEM((LAT, ROWS), BF16),
            pltpu.VMEM((2, ROWS, HALF), BF16),
            pltpu.VMEM((ROWS, LAT), BF16),
            pltpu.VMEM((2, 2, ROWS, QUARTER), BF16),
            pltpu.VMEM((2, 2, ROWS, QUARTER), BF16),
            pltpu.VMEM((2, 2, ROWS, QUARTER), BF16),
            pltpu.VMEM((2, 32, OWN, QUARTER), BF16),
            pltpu.VMEM((2, DEPTH, OWN, QUARTER), BF16),
            pltpu.VMEM((LAT, D), BF16),
            pltpu.VMEM((D, LAT), BF16),
            pltpu.VMEM((2, OWN, HALF), F32),
            pltpu.SemaphoreType.DMA((4,)),
            pltpu.SemaphoreType.DMA((2,)),
            pltpu.SemaphoreType.DMA((6,)),
            pltpu.SemaphoreType.DMA((6,)),
            pltpu.SemaphoreType.DMA((7,)),
            pltpu.SemaphoreType.DMA((7,)),
        ],
        compiler_params=pltpu.CompilerParams(
            collective_id=0, has_side_effects=True, vmem_limit_bytes=40 * 2**20
        ),
        cost_estimate=pl.CostEstimate(
            flops=10 * ROWS * D * LAT, bytes_accessed=5 * 2**20, transcendentals=0
        ),
        name="sae_backward",
    )(passages, enc_weight, enc_bias.reshape(1, LAT), dec_weight, dec_bias.reshape(1, D), active)
    return genc, geb.reshape(LAT), gdec, gdb.reshape(D), gin


def solution(mesh):
    split = P(None, ("wide", "sub"))
    rows = P(("wide", "sub"), None)
    line = P(("wide", "sub"))
    return jax.shard_map(
        per_device,
        mesh=mesh,
        in_specs=(P("sub", None), split, line, rows, P(), split),
        out_specs=(split, line, rows, P(), P("sub", None)),
        check_vma=False,
    )
```

time: 175 us -> 74.9 us (0.43)
  blocking collectives: 103 us -> 0 us
  Pallas kernels: 0 us -> 64.5 us
  waiting for transfers between devices: 29.1 us -> 0 us
  starting transfers between devices: 16.2 us -> 0 us
  matrix products: 7.01 us -> 0 us
  other arithmetic: 6.09 us -> 0 us
  local copies, waits for them, and re-layouts: 12.7 us -> 9.35 us
    all_to_all x5 -> x0, blocking collectives: 103 us -> none  [the longest x3 51.8 us: from_everyone(): return lax.all_to_all(copies, axis, split_axis=0, concat_axis=0, tiled=True)]
    pallas_call x0 -> x1, Pallas kernels: none -> 64.5 us  [per_device(): pl.pallas_call(kernel, out_shape=(jax.ShapeDtypeStruct((D, LAT), BF16), j...]
    all_to_all x3 -> x0, waiting for transfers between devices: 29.1 us -> none  [the longest x2 19.6 us: summed_on_arrival(): lax.all_to_all(blocks, axis, split_axis=0, concat_axis=0, tiled=True)]
    all_to_all x3 -> x0, starting transfers between devices: 16.2 us -> none  [the longest x2 11.5 us: summed_on_arrival(): lax.all_to_all(blocks, axis, split_axis=0, concat_axis=0, tiled=True)]
    dot_general x6 -> x0, matrix products: 7.01 us -> none  [the longest x1 1.43 us: per_device(): lax.dot_general(codes, resid, (((0,), (0,)), ((), ())), preferred_element...]
    another operation x3 -> x0, local copies, waits for them, and re-layouts: 6.73 us -> none  [the longest x2 4.19 us: split_up(): array.reshape(*dims[:dim], count, dims[dim] // count, *dims[dim + 1:])]
    unnamed x20 -> x17, local copies, waits for them, and re-layouts: 2.67 us -> 9.35 us
    reduce_sum x5 -> x0, other arithmetic: 3.63 us -> none  [the longest x1 2.1 us: per_device(): grad_dec_bias = jnp.sum(resid.astype(jnp.float32), axis=0)]
  transfers between devices with their start and end apart: 3 -> 0, of which waited for: 3 -> 0; matrix products, arithmetic and copies ran while one was open for 2% -> 0% of each run, Pallas kernels for 0% -> 0%
where the time goes in v1:
time: 74.9 us; the launch traced here: 74.5 us
  Pallas kernels  64.5 us (86%)
  local copies, waits for them, and re-layouts  9.35 us (12%)
    pallas_call x1, Pallas kernels, per_device(): pl.pallas_call(kernel, out_shape=(jax.ShapeDtypeStruct((D, LAT), BF16), j...  64.5 us
    unnamed x17, local copies, waits for them, and re-layouts  9.35 us

profile of v1, /device:TPU:1, one launch (start us, length us, event | category | flops | bytes accessed | tf_op | source)
XLA Modules:
  0.0 74.5 jit_solution(7346825738110201480)
XLA Ops:
  0.6 0.0 copy-start.5
  0.6 0.7 copy-done.5
  1.3 0.0 copy-start
  1.3 1.2 %copy-done = bf16[1024,512]{1,0:T(8,128)(2,1)S(1)} copy-done((bf16[1024,512]{1,0:T(8,128)(2,1)S(1)}, bf16[1024,512]{1,0:T(8,128)(2,1)}, u32[]{:S(2)}) %copy-start) | copy-done | bytes 1048600
  2.5 0.0 copy-start.1
  2.5 1.2 %copy-done.1 = bf16[512,1024]{1,0:T(8,128)(2,1)S(1)} copy-done((bf16[512,1024]{1,0:T(8,128)(2,1)S(1)}, bf16[512,1024]{1,0:T(8,128)(2,1)}, u32[]{:S(2)}) %copy-start.1) | copy-done | bytes 1048600
  3.8 0.0 copy-start.2
  3.8 1.0 %copy-done.2 = s32[256,512]{1,0:T(8,128)S(1)} copy-done((s32[256,512]{1,0:T(8,128)S(1)}, s32[256,512]{1,0:T(8,128)}, u32[]{:S(2)}) %copy-start.2) | copy-done | bytes 524312
  4.8 0.0 copy-start.3
  4.8 0.8 %copy-done.3 = bf16[16,1024]{1,0:T(8,128)(2,1)S(1)} copy-done((bf16[16,1024]{1,0:T(8,128)(2,1)S(1)}, bf16[16,1024]{1,0:T(8,128)(2,1)}, u32[]{:S(2)}) %copy-start.3) | copy-done | bytes 32792
  5.6 0.0 copy-start.4
  5.6 0.7 copy-done.4
  6.3 64.5 %sae_backward.1 = (bf16[1024,512]{1,0:T(8,128)(2,1)S(1)}, f32[1,512]{1,0:T(1,128)S(1)}, bf16[512,1024]{1,0:T(8,128)(2,1)S(1)}, f32[1,1024]{1,0:T(1,128)S(1)}, f32[16,1024]{1,0:T(8,128)S(1)}) custom-call(bf16[16,1024]{1,0:T(8,128)(2,1)S(1)} %copy-done.3, bf16[1024,512]{1,0:T(8,128)(2,1)S(1)} %copy-done, f32[1,512]{1,0:T(1,128)S(1)} %bitcast.7, ...), custom_call_target="tpu_custom_call" | custom-call | flops 1342177280 | bytes 5242880 | tf_op jit(solution)/shard_map/sae_backward/pallas_call | solution.py:211
  70.7 1.0 %copy.16 = bf16[1024,512]{1,0:T(8,128)(2,1)} copy(bf16[1024,512]{1,0:T(8,128)(2,1)S(1)} %get-tuple-element.20) | data formatting | bytes 2097152
  71.7 0.6 copy.17
  72.3 1.0 %copy.18 = bf16[512,1024]{1,0:T(8,128)(2,1)} copy(bf16[512,1024]{1,0:T(8,128)(2,1)S(1)} %get-tuple-element.22) | data formatting | bytes 2097152
  73.3 0.6 copy.19
  73.9 0.6 copy.20
Async XLA Ops:
  0.6 0.7 copy-start.5
  1.3 1.2 %copy-start = (bf16[1024,512]{1,0:T(8,128)(2,1)S(1)}, bf16[1024,512]{1,0:T(8,128)(2,1)}, u32[]{:S(2)}) copy-start(bf16[1024,512]{1,0:T(8,128)(2,1)} %enc_in.1) | copy-start | bytes 3145732
  2.5 1.2 %copy-start.1 = (bf16[512,1024]{1,0:T(8,128)(2,1)S(1)}, bf16[512,1024]{1,0:T(8,128)(2,1)}, u32[]{:S(2)}) copy-start(bf16[512,1024]{1,0:T(8,128)(2,1)} %dec_in.1) | copy-start | bytes 3145732
  3.8 1.0 %copy-start.2 = (s32[256,512]{1,0:T(8,128)S(1)}, s32[256,512]{1,0:T(8,128)}, u32[]{:S(2)}) copy-start(s32[256,512]{1,0:T(8,128)} %act_in.1) | copy-start | bytes 1572868
  4.8 0.8 %copy-start.3 = (bf16[16,1024]{1,0:T(8,128)(2,1)S(1)}, bf16[16,1024]{1,0:T(8,128)(2,1)}, u32[]{:S(2)}) copy-start(bf16[16,1024]{1,0:T(8,128)(2,1)} %pas_in.1) | copy-start | bytes 98308
  5.6 0.7 copy-start.4

commit v2 on v1

--- a/solution.py
+++ b/solution.py
@@ -28,9 +28,9 @@
 
 
 def kernel(
-    pas_in, enc_in, eb, dec_in, db, act_in,
+    pas_in, enc_in, eb_in, dec_in, db_in, act_in,
     genc_out, geb_out, gdec_out, gdb_out, gin_out,
-    enc, dec, act, every, every_t, pre, codes, codes_t, resid, dpre,
+    enc, dec, act, eb, db, every, every_t, pre, codes, codes_t, resid, dpre,
     swap_out, swap_in, parts, rows_in, rows_z, gdec, genc, final,
     load_sem, store_sem, send_sem, recv_sem, swap_send, swap_recv,
 ):
@@ -62,7 +62,9 @@
         ),
         pltpu.make_async_copy(enc_in, enc, load_sem.at[1]),
         pltpu.make_async_copy(act_in, act, load_sem.at[2]),
-        pltpu.make_async_copy(dec_in, dec, load_sem.at[3]),
+        pltpu.make_async_copy(eb_in, eb, load_sem.at[3]),
+        pltpu.make_async_copy(dec_in, dec, load_sem.at[4]),
+        pltpu.make_async_copy(db_in, db, load_sem.at[5]),
     ]
     for load in loads:
         load.start()
@@ -75,6 +77,8 @@
     loads[0].wait()
     pl.semaphore_wait(barrier, len(greeted))
 
+    pending = []
+
     def send(src, dst, k, peer):
         pltpu.make_async_remote_copy(
             src_ref=src, dst_ref=dst, send_sem=send_sem.at[k], recv_sem=recv_sem.at[k],
@@ -93,14 +97,16 @@
             device_id=sibling, device_id_type=MESH,
         )
         copy.start()
+        pending.append(copy.wait_send)
         return copy
 
     def gather(array, k, swap_k):
         for s in others:
             send(array.at[c, mine], array.at[c, mine], k, (wide, s))
         rest = array.at[c, pl.ds(0, ROWS - OWN)]
+        pending.append(lambda: sent(rest, k))
         arrived(rest, k)
-        return swap(array.at[c], array.at[c], swap_k), rest
+        return swap(array.at[c], array.at[c], swap_k)
 
     def half(h):
         return pl.ds(pl.multiple_of(h * HALF, HALF), HALF)
@@ -126,7 +132,7 @@
                 peer = (wide if t else zn * 2 + c, s)
                 send(parts.at[i, t, rows], rows_in.at[i, slot], k, peer)
         rows_in[i, slot] = parts[i, 1, mine]
-        return swaps
+        pending.append(lambda: sent(rows_in.at[i, pl.ds(0, 31)], k))
 
     def pieces_along_z(i):
         k = 2 + 2 * i
@@ -137,6 +143,7 @@
         rows_z[i, z] = total.astype(BF16)
         for peer in z_peers:
             send(rows_z.at[i, z], rows_z.at[i, z], k + 1, peer)
+        pending.append(lambda: sent(rows_z.at[i, pl.ds(0, 15)], k + 1))
 
     def sum_along_z(i, zq):
         total = rows_z[i, zq].astype(F32)
@@ -144,22 +151,16 @@
             total = total + rows_z[i, 2 * n + zq].astype(F32)
         return total
 
-    def reduce_sent(i, swaps):
-        for copy in swaps:
-            copy.wait_send()
-        sent(rows_in.at[i, pl.ds(0, 31)], 2 + 2 * i)
-        sent(rows_z.at[i, pl.ds(0, 15)], 3 + 2 * i)
-
-    passages_swap, passages_rest = gather(every, 0, 0)
+    passages_swap = gather(every, 0, 0)
     loads[1].wait()
     pre[...] = dot_nn(every[c], enc[half(c), :])
-    loads[2].wait()
-    loads[3].wait()
+    for load in loads[2:]:
+        load.wait()
     passages_swap.wait_recv()
     both = pre[...] + dot_nn(every[oc], enc[half(oc), :]) + eb[...]
     codes[...] = (act[...].astype(F32) * both).astype(BF16)
 
-    swaps_0 = reduce_out(0, lambda q: dot_nn(codes[...], dec[:, quarter(q)]))
+    reduce_out(0, lambda q: dot_nn(codes[...], dec[:, quarter(q)]))
     codes_t[...] = codes[...].T
     pieces_along_z(0)
     every_t[0] = every[0].T
@@ -169,60 +170,67 @@
         recon = sum_along_z(0, zq) + db[:, quarter(c * 2 + zq)]
         columns = pl.ds(zq * QUARTER, QUARTER)
         resid[c, mine, columns] = (recon - every[c, mine, columns].astype(F32)).astype(BF16)
-    resid_swap, resid_rest = gather(resid, 1, 1)
+    resid_swap = gather(resid, 1, 1)
     pre[...] = dot_nt(resid[c], dec[:, half(c)])
     resid_swap.wait_recv()
     back = pre[...] + dot_nt(resid[oc], dec[:, half(oc)])
     dpre[...] = (act[...].astype(F32) * back).astype(BF16)
 
-    swaps_1 = reduce_out(1, lambda q: dot_nt(dpre[...], enc[quarter(q), :]))
-    stores = []
+    reduce_out(1, lambda q: dot_nt(dpre[...], enc[quarter(q), :]))
     for h in range(2):
         gdec[:, pl.ds(h * HALF, HALF)] = dot_nn(codes_t[...], resid[h]).astype(BF16)
         gdb_out[:, pl.ds(h * HALF, HALF)] = jnp.sum(resid[h].astype(F32), axis=0, keepdims=True)
-    stores.append(pltpu.make_async_copy(gdec, gdec_out, store_sem.at[0]))
+    stores = [pltpu.make_async_copy(gdec, gdec_out, store_sem.at[0])]
     stores[0].start()
+    pending.append(stores[0].wait)
     for h in range(2):
         genc[pl.ds(h * HALF, HALF), :] = dot_nn(every_t[h], dpre[...]).astype(BF16)
     stores.append(pltpu.make_async_copy(genc, genc_out, store_sem.at[1]))
     stores[1].start()
+    pending.append(stores[1].wait)
     geb_out[...] = jnp.sum(dpre[...].astype(F32), axis=0, keepdims=True)
     pieces_along_z(1)
-    passages_swap.wait_send()
-    resid_swap.wait_send()
-    sent(passages_rest, 0)
-    sent(resid_rest, 1)
-    reduce_sent(0, swaps_0)
     arrived(rows_z.at[1, pl.ds(0, 15)], 5)
     for zq in range(2):
         final[c, :, pl.ds(zq * QUARTER, QUARTER)] = sum_along_z(1, zq)
     final_swap = swap(final.at[c], final.at[c], 6)
-    reduce_sent(1, swaps_1)
-    for store in stores:
-        store.wait()
-    final_swap.wait()
+    final_swap.wait_recv()
+    for wait in pending:
+        wait()
     for h in range(2):
         gin_out[:, pl.ds(h * HALF, HALF)] = final[h] - resid[h, mine].astype(F32)
+
+
+def place(genc_in, geb_in, gdec_in, gdb_in, gin_in, genc, geb, gdec, gdb, gin, sem):
+    pairs = [(genc_in, genc), (gdec_in, gdec), (gin_in, gin), (geb_in, geb), (gdb_in, gdb)]
+    copies = [pltpu.make_async_copy(a, b, sem.at[i]) for i, (a, b) in enumerate(pairs)]
+    for copy in copies:
+        copy.start()
+    for copy in copies:
+        copy.wait()
 
 
 def per_device(passages, enc_weight, enc_bias, dec_weight, dec_bias, active):
     anywhere = pl.BlockSpec(memory_space=pl.ANY)
     vmem = pl.BlockSpec(memory_space=pltpu.VMEM)
-    genc, geb, gdec, gdb, gin = pl.pallas_call(
+    shapes = (
+        jax.ShapeDtypeStruct((D, LAT), BF16),
+        jax.ShapeDtypeStruct((1, LAT), F32),
+        jax.ShapeDtypeStruct((LAT, D), BF16),
+        jax.ShapeDtypeStruct((1, D), F32),
+        jax.ShapeDtypeStruct((OWN, D), F32),
+    )
+    results = pl.pallas_call(
         kernel,
-        out_shape=(
-            jax.ShapeDtypeStruct((D, LAT), BF16),
-            jax.ShapeDtypeStruct((1, LAT), F32),
-            jax.ShapeDtypeStruct((LAT, D), BF16),
-            jax.ShapeDtypeStruct((1, D), F32),
-            jax.ShapeDtypeStruct((OWN, D), F32),
-        ),
-        in_specs=[anywhere, anywhere, vmem, anywhere, vmem, anywhere],
+        out_shape=shapes,
+        in_specs=[pl.BlockSpec(memory_space=pltpu.HBM)] * 6,
         out_specs=(anywhere, vmem, anywhere, vmem, vmem),
         scratch_shapes=[
             pltpu.VMEM((D, LAT), BF16),
             pltpu.VMEM((LAT, D), BF16),
             pltpu.VMEM((ROWS, LAT), jnp.int32),
+            pltpu.VMEM((1, LAT), F32),
+            pltpu.VMEM((1, D), F32),
             pltpu.VMEM((2, ROWS, HALF), BF16),
             pltpu.VMEM((2, HALF, ROWS), BF16),
             pltpu.VMEM((ROWS, LAT), F32),
@@ -238,7 +246,7 @@
             pltpu.VMEM((LAT, D), BF16),
             pltpu.VMEM((D, LAT), BF16),
             pltpu.VMEM((2, OWN, HALF), F32),
-            pltpu.SemaphoreType.DMA((4,)),
+            pltpu.SemaphoreType.DMA((6,)),
             pltpu.SemaphoreType.DMA((2,)),
             pltpu.SemaphoreType.DMA((6,)),
             pltpu.SemaphoreType.DMA((6,)),
@@ -246,13 +254,22 @@
             pltpu.SemaphoreType.DMA((7,)),
         ],
         compiler_params=pltpu.CompilerParams(
-            collective_id=0, has_side_effects=True, vmem_limit_bytes=40 * 2**20
+            collective_id=0, has_side_effects=True, vmem_limit_bytes=63 * 2**20
         ),
         cost_estimate=pl.CostEstimate(
             flops=10 * ROWS * D * LAT, bytes_accessed=5 * 2**20, transcendentals=0
         ),
         name="sae_backward",
     )(passages, enc_weight, enc_bias.reshape(1, LAT), dec_weight, dec_bias.reshape(1, D), active)
+    genc, geb, gdec, gdb, gin = pl.pallas_call(
+        place,
+        out_shape=shapes,
+        in_specs=[anywhere] * 5,
+        out_specs=[anywhere] * 5,
+        scratch_shapes=[pltpu.SemaphoreType.DMA((5,))],
+        compiler_params=pltpu.CompilerParams(vmem_limit_bytes=63 * 2**20),
+        name="place",
+    )(*results)
     return genc, geb.reshape(LAT), gdec, gdb.reshape(D), gin
 
 

time: 74.9 us -> 132 us (1.76)
  Pallas kernels: 64.5 us -> 131 us
  local copies, waits for them, and re-layouts: 9.35 us -> 0 us
    pallas_call x1 -> x2, Pallas kernels: 64.5 us -> 131 us  [the longest x1 66.8 us: per_device(): pl.pallas_call(place, out_shape=shapes, in_specs=[anywhere] * 5, out_spec...]
    unnamed x17 -> x0, local copies, waits for them, and re-layouts: 9.35 us -> none
where the time goes in v2:
time: 132 us
  Pallas kernels  131 us (99%)
    pallas_call x1, Pallas kernels, per_device(): pl.pallas_call(place, out_shape=shapes, in_specs=[anywhere] * 5, out_spec...  66.8 us
    pallas_call x1, Pallas kernels, per_device(): pl.pallas_call(kernel, out_shape=shapes, in_specs=[pl.BlockSpec(memory_sp...  64.3 us

profile of v2, /device:TPU:1, one launch (start us, length us, event | category | flops | bytes accessed | tf_op | source)
XLA Modules:
  0.0 131.8 jit_solution(397511248523265769)
XLA Ops:
  0.6 64.3 %sae_backward.1 = (bf16[1024,512]{1,0:T(8,128)(2,1)}, f32[1,512]{1,0:T(1,128)}, bf16[512,1024]{1,0:T(8,128)(2,1)}, f32[1,1024]{1,0:T(1,128)}, f32[16,1024]{1,0:T(8,128)}) custom-call(bf16[16,1024]{1,0:T(8,128)(2,1)} %pas_in.1, bf16[1024,512]{1,0:T(8,128)(2,1)} %enc_in.1, f32[1,512]{1,0:T(1,128)} %bitcast.6, bf16[512,1024]{1,0:T(8,128)(2,1)} %dec_in.1, ...), custom_call_target="tpu_custom_call" | custom-call | flops 1342177280 | bytes 5242880 | tf_op jit(solution)/shard_map/sae_backward/pallas_call | solution.py:223
  64.9 66.8 %place.1 = (bf16[1024,512]{1,0:T(8,128)(2,1)}, f32[1,512]{1,0:T(1,128)}, bf16[512,1024]{1,0:T(8,128)(2,1)}, f32[1,1024]{1,0:T(1,128)}, f32[16,1024]{1,0:T(8,128)}) custom-call(bf16[1024,512]{1,0:T(8,128)(2,1)} %get-tuple-element.15.genc_in, f32[1,512]{1,0:T(1,128)} %get-tuple-element.16.geb_in, bf16[512,1024]{1,0:T(8,128)(2,1)} %get-tuple-element.17.gdec_in, ...), custom_call_target="tpu_custom_call" | custom-call | tf_op jit(solution)/shard_map/place/pallas_call | solution.py:264

commit v3 on v2

--- a/solution.py
+++ b/solution.py
@@ -31,8 +31,8 @@
     pas_in, enc_in, eb_in, dec_in, db_in, act_in,
     genc_out, geb_out, gdec_out, gdb_out, gin_out,
     enc, dec, act, eb, db, every, every_t, pre, codes, codes_t, resid, dpre,
-    swap_out, swap_in, parts, rows_in, rows_z, gdec, genc, final,
-    load_sem, store_sem, send_sem, recv_sem, swap_send, swap_recv,
+    swap_out, swap_in, parts, rows_in, rows_z, final,
+    load_sem, send_sem, recv_sem, swap_send, swap_recv,
 ):
     wide, sub = lax.axis_index("wide"), lax.axis_index("sub")
     z, c = wide // 2, wide % 2
@@ -178,16 +178,10 @@
 
     reduce_out(1, lambda q: dot_nt(dpre[...], enc[quarter(q), :]))
     for h in range(2):
-        gdec[:, pl.ds(h * HALF, HALF)] = dot_nn(codes_t[...], resid[h]).astype(BF16)
+        gdec_out[:, pl.ds(h * HALF, HALF)] = dot_nn(codes_t[...], resid[h]).astype(BF16)
         gdb_out[:, pl.ds(h * HALF, HALF)] = jnp.sum(resid[h].astype(F32), axis=0, keepdims=True)
-    stores = [pltpu.make_async_copy(gdec, gdec_out, store_sem.at[0])]
-    stores[0].start()
-    pending.append(stores[0].wait)
     for h in range(2):
-        genc[pl.ds(h * HALF, HALF), :] = dot_nn(every_t[h], dpre[...]).astype(BF16)
-    stores.append(pltpu.make_async_copy(genc, genc_out, store_sem.at[1]))
-    stores[1].start()
-    pending.append(stores[1].wait)
+        genc_out[pl.ds(h * HALF, HALF), :] = dot_nn(every_t[h], dpre[...]).astype(BF16)
     geb_out[...] = jnp.sum(dpre[...].astype(F32), axis=0, keepdims=True)
     pieces_along_z(1)
     arrived(rows_z.at[1, pl.ds(0, 15)], 5)
@@ -213,6 +207,9 @@
 def per_device(passages, enc_weight, enc_bias, dec_weight, dec_bias, active):
     anywhere = pl.BlockSpec(memory_space=pl.ANY)
     vmem = pl.BlockSpec(memory_space=pltpu.VMEM)
+    arrays = (
+        passages, enc_weight, enc_bias.reshape(1, LAT), dec_weight, dec_bias.reshape(1, D), active
+    )
     shapes = (
         jax.ShapeDtypeStruct((D, LAT), BF16),
         jax.ShapeDtypeStruct((1, LAT), F32),
@@ -222,9 +219,9 @@
     )
     results = pl.pallas_call(
         kernel,
-        out_shape=shapes,
+        out_shape=[pltpu.VMEM(s.shape, s.dtype) for s in shapes],
         in_specs=[pl.BlockSpec(memory_space=pltpu.HBM)] * 6,
-        out_specs=(anywhere, vmem, anywhere, vmem, vmem),
+        out_specs=[vmem] * 5,
         scratch_shapes=[
             pltpu.VMEM((D, LAT), BF16),
             pltpu.VMEM((LAT, D), BF16),
@@ -243,33 +240,30 @@
             pltpu.VMEM((2, 2, ROWS, QUARTER), BF16),
             pltpu.VMEM((2, 32, OWN, QUARTER), BF16),
             pltpu.VMEM((2, DEPTH, OWN, QUARTER), BF16),
-            pltpu.VMEM((LAT, D), BF16),
-            pltpu.VMEM((D, LAT), BF16),
             pltpu.VMEM((2, OWN, HALF), F32),
             pltpu.SemaphoreType.DMA((6,)),
-            pltpu.SemaphoreType.DMA((2,)),
             pltpu.SemaphoreType.DMA((6,)),
             pltpu.SemaphoreType.DMA((6,)),
             pltpu.SemaphoreType.DMA((7,)),
             pltpu.SemaphoreType.DMA((7,)),
         ],
         compiler_params=pltpu.CompilerParams(
-            collective_id=0, has_side_effects=True, vmem_limit_bytes=63 * 2**20
+            collective_id=0, has_side_effects=True, vmem_limit_bytes=40 * 2**20
         ),
         cost_estimate=pl.CostEstimate(
             flops=10 * ROWS * D * LAT, bytes_accessed=5 * 2**20, transcendentals=0
         ),
         name="sae_backward",
-    )(passages, enc_weight, enc_bias.reshape(1, LAT), dec_weight, dec_bias.reshape(1, D), active)
+    )(*(pltpu.with_memory_space_constraint(a, pltpu.HBM) for a in arrays))
     genc, geb, gdec, gdb, gin = pl.pallas_call(
         place,
         out_shape=shapes,
-        in_specs=[anywhere] * 5,
+        in_specs=[vmem] * 5,
         out_specs=[anywhere] * 5,
         scratch_shapes=[pltpu.SemaphoreType.DMA((5,))],
-        compiler_params=pltpu.CompilerParams(vmem_limit_bytes=63 * 2**20),
+        compiler_params=pltpu.CompilerParams(vmem_limit_bytes=2**18),
         name="place",
-    )(*results)
+    )(*(pltpu.with_memory_space_constraint(a, pltpu.VMEM) for a in results))
     return genc, geb.reshape(LAT), gdec, gdb.reshape(D), gin
 
 

time: 132 us -> 65.8 us (0.50)
  Pallas kernels: 131 us -> 65 us
    pallas_call x2, Pallas kernels: 131 us -> 65 us  [the longest x1 63.6 us: per_device(): pl.pallas_call(kernel, out_shape=[pltpu.VMEM(s.shape, s.dtype) for s in s...]
where the time goes in v3:
time: 65.8 us; the launch traced here: 65.6 us
  Pallas kernels  65 us (99%)
    pallas_call x1, Pallas kernels, per_device(): pl.pallas_call(kernel, out_shape=[pltpu.VMEM(s.shape, s.dtype) for s in s...  63.6 us
    pallas_call x1, Pallas kernels, per_device(): pl.pallas_call(place, out_shape=shapes, in_specs=[vmem] * 5, out_specs=[a...  1.37 us

profile of v3, /device:TPU:1, one launch (start us, length us, event | category | flops | bytes accessed | tf_op | source)
XLA Modules:
  0.0 65.6 jit_solution(14332666703519813773)
XLA Ops:
  0.6 63.6 %sae_backward.1 = (bf16[1024,512]{1,0:T(8,128)(2,1)S(1)}, f32[1,512]{1,0:T(1,128)S(1)}, bf16[512,1024]{1,0:T(8,128)(2,1)S(1)}, f32[1,1024]{1,0:T(1,128)S(1)}, f32[16,1024]{1,0:T(8,128)S(1)}) custom-call(bf16[16,1024]{1,0:T(8,128)(2,1)} %pas_in.1, bf16[1024,512]{1,0:T(8,128)(2,1)} %enc_in.1, f32[1,512]{1,0:T(1,128)} %bitcast.6, bf16[512,1024]{1,0:T(8,128)(2,1)} %dec_in.1, ...), custom_call_target="tpu_custom_call" | custom-call | flops 1342177280 | bytes 5242880 | tf_op jit(solution)/shard_map/sae_backward/pallas_call | solution.py:220
  64.3 1.4 %place.1 = (bf16[1024,512]{1,0:T(8,128)(2,1)}, f32[1,512]{1,0:T(1,128)}, bf16[512,1024]{1,0:T(8,128)(2,1)}, f32[1,1024]{1,0:T(1,128)}, f32[16,1024]{1,0:T(8,128)}) custom-call(bf16[1024,512]{1,0:T(8,128)(2,1)S(1)} %get-tuple-element.15.genc_in, f32[1,512]{1,0:T(1,128)S(1)} %get-tuple-element.16.geb_in, bf16[512,1024]{1,0:T(8,128)(2,1)S(1)} %get-tuple-element.17.gdec_in, ...), custom_call_target="tpu_custom_call" | custom-call | tf_op jit(solution)/shard_map/place/pallas_call | solution.py:258

commit v4 on v3

v4 whole, which is shorter than its diff:
```python
import jax
import jax.numpy as jnp
from jax import lax
from jax.experimental import pallas as pl
from jax.experimental.pallas import tpu as pltpu
from jax.sharding import PartitionSpec as P

MESH = pl.DeviceIdType.MESH
BF16 = jnp.bfloat16
F32 = jnp.float32
ROWS, D, LAT = 256, 1024, 512
OWN, HALF, QUARTER = 16, 512, 256
SIDE, DEPTH = 4, 16


def ring(d, n):
    return min(d, n - d)


OFFSETS = sorted(
    ((dx, dy) for dx in range(SIDE) for dy in range(SIDE)),
    key=lambda o: -ring(o[0], SIDE) - ring(o[1], SIDE),
)
BACK = [OFFSETS.index((-dx % SIDE, -dy % SIDE)) for dx, dy in OFFSETS]
PEERS = len(OFFSETS) - 1
FORWARD = ((11, 16), (8, 11), (5, 8), (3, 5), (1, 3), (0, 1))
CHUNKS = ((0, 5), (5, 11), (11, 16))
Z_STEPS = sorted(range(1, DEPTH), key=lambda d: -ring(d, DEPTH))


def blocks(first, last):
    return pl.ds(first * OWN, (last - first) * OWN)


def dot_nt(a, b):
    return lax.dot_general(a, b, (((1,), (1,)), ((), ())), preferred_element_type=F32)


def dot_nn(a, b):
    return jnp.dot(a, b, preferred_element_type=F32)


def kernel(
    pas_in, enc_in, eb_in, dec_in, db_in, act_in,
    genc_out, geb_out, gdec_out, gdb_out, gin_out,
    enc, dec, act, eb, db, every, every_t, pre, codes, codes_t, resid, dpre,
    swap_out, swap_in, parts, rows_in, rows_z, block_sums, final,
    load_sem, send_sem, block_sem, piece_sem, z_sem, swap_send, swap_recv, near_sem,
):
    wide, sub = lax.axis_index("wide"), lax.axis_index("sub")
    z, c = wide // 2, wide % 2
    x, y = sub // SIDE, sub % SIDE
    zp = z % 2
    oc = 1 - c
    mine = blocks(PEERS, PEERS + 1)

    def along_z(d):
        return (((z + d) % DEPTH) * 2 + c, sub)

    subs = [((x + dx) % SIDE) * SIDE + (y + dy) % SIDE for dx, dy in OFFSETS]
    other_plane = (z + 1 - 2 * zp) * 2 + c
    sibling = (z * 2 + oc, sub)

    def half(h):
        return pl.ds(pl.multiple_of(h * HALF, HALF), HALF)

    def quarter(q):
        return pl.ds(pl.multiple_of(q * QUARTER, QUARTER), QUARTER)

    own_load = pltpu.make_async_copy(pas_in.at[:, half(c)], every.at[c, mine], load_sem.at[0])
    enc_load = pltpu.make_async_copy(enc_in, enc, load_sem.at[1])
    loads = [
        pltpu.make_async_copy(eb_in, eb, load_sem.at[2]),
        pltpu.make_async_copy(dec_in, dec, load_sem.at[3]),
        pltpu.make_async_copy(db_in, db, load_sem.at[4]),
    ]

    barrier = pltpu.get_barrier_semaphore()
    own_load.start()
    greeted = [(wide, s) for s in subs[:PEERS]] + [sibling, along_z(1), along_z(DEPTH - 1)]
    for peer in greeted:
        pl.semaphore_signal(barrier, inc=1, device_id=peer, device_id_type=MESH)
    own_load.wait()
    pl.semaphore_wait(barrier, len(greeted))

    def tell(step):
        for d in (1 << step, DEPTH - (1 << step)):
            pl.semaphore_signal(
                near_sem.at[step], inc=1, device_id=along_z(d), device_id_type=MESH
            )

    def told(step):
        pl.semaphore_wait(near_sem.at[step], 2)

    pending = []

    def send(src, dst, k, recv, peer):
        pltpu.make_async_remote_copy(
            src_ref=src, dst_ref=dst, send_sem=send_sem.at[k], recv_sem=recv,
            device_id=peer, device_id_type=MESH,
        ).start()

    def wait(ref, sem):
        pltpu.make_async_copy(ref, ref, sem).wait()

    def forward(array, i, first, last):
        ref = array.at[c, ..., blocks(first, last), :]
        pltpu.make_async_remote_copy(
            src_ref=ref, dst_ref=ref, send_sem=swap_send.at[i], recv_sem=swap_recv.at[i],
            device_id=sibling, device_id_type=MESH,
        ).start()

    def forwarded(array, i):
        wait(array.at[oc], swap_recv.at[i])
        pending.append(lambda: wait(array.at[c], swap_send.at[i]))

    def reduce_out(i, part):
        swaps = []
        for n, (first, last) in enumerate(CHUNKS):
            rows = blocks(first, last)
            for t in range(2):
                q = oc * 2 + (zp if t else 1 - zp)
                swap_out[i, t, rows] = part(q, rows).astype(BF16)
            swap = pltpu.make_async_remote_copy(
                src_ref=swap_out.at[i, :, rows], dst_ref=swap_in.at[i, :, rows],
                send_sem=swap_send.at[2 + 3 * i + n], recv_sem=swap_recv.at[2 + 3 * i + n],
                device_id=sibling, device_id_type=MESH,
            )
            swap.start()
            swaps.append(swap)
        for swap, (first, last) in zip(swaps, CHUNKS):
            rows = blocks(first, last)
            own = [part(c * 2 + (zp if t else 1 - zp), rows) for t in range(2)]
            swap.wait_recv()
            for t in range(2):
                parts[i, t, rows] = (own[t] + swap_in[i, t, rows].astype(F32)).astype(BF16)
                for k in range(first, last):
                    if t and k == PEERS:
                        continue
                    send(
                        parts.at[i, t, blocks(k, k + 1)], rows_in.at[i, t, BACK[k]],
                        2 + 2 * i + t, piece_sem.at[i, t], (wide if t else other_plane, subs[k]),
                    )
            pending.append(swap.wait_send)
        rows_in[i, 1, PEERS] = parts[i, 1, mine]

        pending.append(lambda: wait(parts.at[i, 0], send_sem.at[2 + 2 * i]))
        pending.append(lambda: wait(parts.at[i, 1, blocks(0, PEERS)], send_sem.at[3 + 2 * i]))

    def pieces_in(i, slot):
        wait(rows_in.at[i, 1, pl.ds(0, PEERS)], piece_sem.at[i, 1])
        total = rows_in[i, 1, 0].astype(F32)
        for n in range(1, PEERS + 1):
            total = total + rows_in[i, 1, n].astype(F32)
        wait(rows_in.at[i, 0], piece_sem.at[i, 0])
        for n in range(PEERS + 1):
            total = total + rows_in[i, 0, n].astype(F32)
        rows_z[i, slot] = total.astype(BF16)

    for k in range(PEERS):
        there = every.at[c, blocks(BACK[k], BACK[k] + 1)]
        send(every.at[c, mine], there, 0, block_sem.at[0, BACK[k]], (wide, subs[k]))
    pending.append(lambda: wait(every.at[c, blocks(0, PEERS)], send_sem.at[0]))
    tell(0)
    enc_load.start()
    for k, s in enumerate(subs):
        rows = pl.ds(pl.multiple_of(s * OWN, OWN), OWN)
        pltpu.make_async_copy(act_in.at[rows], act.at[blocks(k, k + 1)], load_sem.at[5]).start()
    for load in loads:
        load.start()
    for n, (first, last) in enumerate(FORWARD):
        for k in range(min(last, PEERS) - 1, first - 1, -1):
            wait(every.at[c, blocks(k, k + 1)], block_sem.at[0, k])
        forward(every, 0, first, last)
        if n == 0:
            told(0)
            tell(1)
    enc_load.wait()
    for load in loads:
        load.wait()
    wait(act, load_sem.at[5])
    pre[...] = dot_nn(every[c], enc[half(c), :]) + eb[...]
    forwarded(every, 0)
    both = pre[...] + dot_nn(every[oc], enc[half(oc), :])
    codes[...] = (act[...].astype(F32) * both).astype(BF16)
    told(1)
    tell(2)

    reduce_out(0, lambda q, rows: dot_nn(codes[rows], dec[:, quarter(q)]))
    codes_t[...] = codes[...].T
    told(2)
    pieces_in(0, z // 2)
    for d in Z_STEPS:
        if d % 2 == 0:
            send(rows_z.at[0, z // 2], rows_z.at[0, z // 2], 6, z_sem.at[0], along_z(d))
    pending.append(lambda: wait(rows_z.at[0, pl.ds(0, DEPTH // 2 - 1)], send_sem.at[6]))
    every_t[0] = every[0].T
    every_t[1] = every[1].T
    wait(rows_z.at[0, pl.ds(0, DEPTH // 2 - 1)], z_sem.at[0])
    recon = rows_z[0, 0].astype(F32)
    for n in range(1, DEPTH // 2):
        recon = recon + rows_z[0, n].astype(F32)
    recon = recon + db[:, quarter(c * 2 + zp)]
    owned = every[c, mine, quarter(zp)].astype(F32)
    resid[c, zp, mine] = (recon - owned).astype(BF16)
    for k in range(PEERS + 1):
        for t in range(2):
            if t and k == PEERS:
                continue
            there = resid.at[c, zp, blocks(BACK[k], BACK[k] + 1)]
            recv = block_sem.at[1 + t, BACK[k]]
            send(resid.at[c, zp, mine], there, 8 if t else 1, recv, (wide if t else other_plane, subs[k]))
    pending.append(lambda: wait(rows_in.at[0, 0], send_sem.at[1]))
    pending.append(lambda: wait(rows_in.at[0, 1, pl.ds(0, PEERS)], send_sem.at[8]))
    for first, last in FORWARD:
        for k in range(last - 1, first - 1, -1):
            if k < PEERS:
                wait(resid.at[c, zp, blocks(k, k + 1)], block_sem.at[2, k])
            wait(resid.at[c, 1 - zp, blocks(k, k + 1)], block_sem.at[1, k])
        forward(resid, 1, first, last)
    back = dot_nt(resid[c, 0], dec[:, quarter(c * 2)])
    pre[...] = back + dot_nt(resid[c, 1], dec[:, quarter(c * 2 + 1)])
    forwarded(resid, 1)
    back = pre[...] + dot_nt(resid[oc, 0], dec[:, quarter(oc * 2)])
    back = back + dot_nt(resid[oc, 1], dec[:, quarter(oc * 2 + 1)])
    dpre[...] = (act[...].astype(F32) * back).astype(BF16)

    reduce_out(1, lambda q, rows: dot_nt(dpre[rows], enc[quarter(q), :]))
    for h in range(2):
        for n in range(2):
            gdec_out[:, quarter(2 * h + n)] = dot_nn(codes_t[...], resid[h, n]).astype(BF16)
        genc_out[half(h), :] = dot_nn(every_t[h], dpre[...]).astype(BF16)
    geb_out[...] = jnp.sum(dpre[...].astype(F32), axis=0, keepdims=True)
    pieces_in(1, z)
    for d in Z_STEPS:
        send(rows_z.at[1, z], rows_z.at[1, z], 7, z_sem.at[1], along_z(d))
    for q in range(4):
        for k, s in enumerate(subs):
            rows = resid[q // 2, q % 2, blocks(k, k + 1)].astype(F32)
            block_sums[pl.ds(s, 1), quarter(q)] = jnp.sum(rows, axis=0, keepdims=True)
    gdb_out[...] = jnp.sum(block_sums[...], axis=0, keepdims=True)
    for end in pending:
        end()
    pending.clear()
    everything = rows_z.at[1, pl.ds(0, DEPTH - 1)]
    wait(everything, z_sem.at[1])
    for zq in range(2):
        total = rows_z[1, zq].astype(F32)
        for n in range(1, DEPTH // 2):
            total = total + rows_z[1, 2 * n + zq].astype(F32)
        final[c, zq] = total
    final_swap = pltpu.make_async_remote_copy(
        src_ref=final.at[c], dst_ref=final.at[c],
        send_sem=swap_send.at[8], recv_sem=swap_recv.at[8],
        device_id=sibling, device_id_type=MESH,
    )
    final_swap.start()
    wait(everything, send_sem.at[7])
    for zq in range(2):
        gin_out[:, quarter(c * 2 + zq)] = final[c, zq] - resid[c, zq, mine].astype(F32)
    final_swap.wait()
    for zq in range(2):
        gin_out[:, quarter(oc * 2 + zq)] = final[oc, zq] - resid[oc, zq, mine].astype(F32)


def place(genc_in, geb_in, gdec_in, gdb_in, gin_in, genc, geb, gdec, gdb, gin, sem):
    pairs = [(gin_in, gin), (geb_in, geb), (gdb_in, gdb)]
    for whole_in, whole in ((genc_in, genc), (gdec_in, gdec)):
        step = whole.shape[0] // 4
        for n in range(4):
            rows = pl.ds(n * step, step)
            pairs.append((whole_in.at[rows], whole.at[rows]))
    copies = [pltpu.make_async_copy(a, b, sem.at[i]) for i, (a, b) in enumerate(pairs)]
    for copy in copies:
        copy.start()
    for copy in copies:
        copy.wait()


def per_device(passages, enc_weight, enc_bias, dec_weight, dec_bias, active):
    anywhere = pl.BlockSpec(memory_space=pl.ANY)
    vmem = pl.BlockSpec(memory_space=pltpu.VMEM)
    arrays = (
        passages, enc_weight, enc_bias.reshape(1, LAT), dec_weight, dec_bias.reshape(1, D), active
    )
    shapes = (
        jax.ShapeDtypeStruct((D, LAT), BF16),
        jax.ShapeDtypeStruct((1, LAT), F32),
        jax.ShapeDtypeStruct((LAT, D), BF16),
        jax.ShapeDtypeStruct((1, D), F32),
        jax.ShapeDtypeStruct((OWN, D), F32),
    )
    results = pl.pallas_call(
        kernel,
        out_shape=[pltpu.VMEM(s.shape, s.dtype) for s in shapes],
        in_specs=[pl.BlockSpec(memory_space=pltpu.HBM)] * 6,
        out_specs=[vmem] * 5,
        scratch_shapes=[
            pltpu.VMEM((D, LAT), BF16),
            pltpu.VMEM((LAT, D), BF16),
            pltpu.VMEM((ROWS, LAT), jnp.int32),
            pltpu.VMEM((1, LAT), F32),
            pltpu.VMEM((1, D), F32),
            pltpu.VMEM((2, ROWS, HALF), BF16),
            pltpu.VMEM((2, HALF, ROWS), BF16),
            pltpu.VMEM((ROWS, LAT), F32),
            pltpu.VMEM((ROWS, LAT), BF16),
            pltpu.VMEM((LAT, ROWS), BF16),
            pltpu.VMEM((2, 2, ROWS, QUARTER), BF16),
            pltpu.VMEM((ROWS, LAT), BF16),
            pltpu.VMEM((2, 2, ROWS, QUARTER), BF16),
            pltpu.VMEM((2, 2, ROWS, QUARTER), BF16),
            pltpu.VMEM((2, 2, ROWS, QUARTER), BF16),
            pltpu.VMEM((2, 2, PEERS + 1, OWN, QUARTER), BF16),
            pltpu.VMEM((2, DEPTH, OWN, QUARTER), BF16),
            pltpu.VMEM((PEERS + 1, D), F32),
            pltpu.VMEM((2, 2, OWN, QUARTER), F32),
            pltpu.SemaphoreType.DMA((6,)),
            pltpu.SemaphoreType.DMA((9,)),
            pltpu.SemaphoreType.DMA((3, PEERS + 1)),
            pltpu.SemaphoreType.DMA((2, 2)),
            pltpu.SemaphoreType.DMA((2,)),
            pltpu.SemaphoreType.DMA((9,)),
            pltpu.SemaphoreType.DMA((9,)),
            pltpu.SemaphoreType.REGULAR((3,)),
        ],
        compiler_params=pltpu.CompilerParams(
            collective_id=0, has_side_effects=True, vmem_limit_bytes=40 * 2**20
        ),
        cost_estimate=pl.CostEstimate(
            flops=10 * ROWS * D * LAT, bytes_accessed=5 * 2**20, transcendentals=0
        ),
        name="sae_backward",
    )(*(pltpu.with_memory_space_constraint(a, pltpu.HBM) for a in arrays))
    genc, geb, gdec, gdb, gin = pl.pallas_call(
        place,
        out_shape=shapes,
        in_specs=[vmem] * 5,
        out_specs=[anywhere] * 5,
        scratch_shapes=[pltpu.SemaphoreType.DMA((11,))],
        compiler_params=pltpu.CompilerParams(vmem_limit_bytes=2**18),
        name="place",
    )(*(pltpu.with_memory_space_constraint(a, pltpu.VMEM) for a in results))
    return genc, geb.reshape(LAT), gdec, gdb.reshape(D), gin


def solution(mesh):
    split = P(None, ("wide", "sub"))
    rows = P(("wide", "sub"), None)
    line = P(("wide", "sub"))
    return jax.shard_map(
        per_device,
        mesh=mesh,
        in_specs=(P("sub", None), split, line, rows, P(), split),
        out_specs=(split, line, rows, P(), P("sub", None)),
        check_vma=False,
    )
```

time: 65.8 us -> 63.8 us (0.970)
  Pallas kernels: 65 us -> 63 us
    pallas_call x1, Pallas kernels: 63.6 us -> 61.6 us  [per_device(): pl.pallas_call(kernel, out_shape=[pltpu.VMEM(s.shape, s.dtype) for s in s...]
where the time goes in v4:
time: 63.8 us; the launch traced here: 63.7 us
  Pallas kernels  63 us (99%)
  between operations  0.64 us (1%)
    pallas_call x1, Pallas kernels, per_device(): pl.pallas_call(kernel, out_shape=[pltpu.VMEM(s.shape, s.dtype) for s in s...  61.6 us
    pallas_call x1, Pallas kernels, per_device(): pl.pallas_call(place, out_shape=shapes, in_specs=[vmem] * 5, out_specs=[a...  1.43 us

profile of v4, /device:TPU:1, one launch (start us, length us, event | category | flops | bytes accessed | tf_op | source)
XLA Modules:
  0.0 63.7 jit_solution(15277654264514756110)
XLA Ops:
  0.6 61.6 %sae_backward.1 = (bf16[1024,512]{1,0:T(8,128)(2,1)S(1)}, f32[1,512]{1,0:T(1,128)S(1)}, bf16[512,1024]{1,0:T(8,128)(2,1)S(1)}, f32[1,1024]{1,0:T(1,128)S(1)}, f32[16,1024]{1,0:T(8,128)S(1)}) custom-call(bf16[16,1024]{1,0:T(8,128)(2,1)} %pas_in.1, bf16[1024,512]{1,0:T(8,128)(2,1)} %enc_in.1, f32[1,512]{1,0:T(1,128)} %bitcast.6, bf16[512,1024]{1,0:T(8,128)(2,1)} %dec_in.1, ...), custom_call_target="tpu_custom_call" | custom-call | flops 1342177280 | bytes 5242880 | tf_op jit(solution)/shard_map/sae_backward/pallas_call | solution.py:293
  62.2 1.4 %place.1 = (bf16[1024,512]{1,0:T(8,128)(2,1)}, f32[1,512]{1,0:T(1,128)}, bf16[512,1024]{1,0:T(8,128)(2,1)}, f32[1,1024]{1,0:T(1,128)}, f32[16,1024]{1,0:T(8,128)}) custom-call(bf16[1024,512]{1,0:T(8,128)(2,1)S(1)} %get-tuple-element.15.genc_in, f32[1,512]{1,0:T(1,128)S(1)} %get-tuple-element.16.geb_in, bf16[512,1024]{1,0:T(8,128)(2,1)S(1)} %get-tuple-element.17.gdec_in, ...), custom_call_target="tpu_custom_call" | custom-call | tf_op jit(solution)/shard_map/place/pallas_call | solution.py:335

commit v5 on v4

--- a/solution.py
+++ b/solution.py
@@ -32,10 +32,6 @@
     return pl.ds(first * OWN, (last - first) * OWN)
 
 
-def dot_nt(a, b):
-    return lax.dot_general(a, b, (((1,), (1,)), ((), ())), preferred_element_type=F32)
-
-
 def dot_nn(a, b):
     return jnp.dot(a, b, preferred_element_type=F32)
 
@@ -43,9 +39,9 @@
 def kernel(
     pas_in, enc_in, eb_in, dec_in, db_in, act_in,
     genc_out, geb_out, gdec_out, gdb_out, gin_out,
-    enc, dec, act, eb, db, every, every_t, pre, codes, codes_t, resid, dpre,
+    enc, enc_t, dec, dec_t, act, eb, db, every, every_t, pre, own, codes, codes_t, resid, dpre,
     swap_out, swap_in, parts, rows_in, rows_z, block_sums, final,
-    load_sem, send_sem, block_sem, piece_sem, z_sem, swap_send, swap_recv, near_sem,
+    load_sem, send_sem, block_sem, piece_sem, z_sem, swap_send, swap_recv, mate_sem, near_sem,
 ):
     wide, sub = lax.axis_index("wide"), lax.axis_index("sub")
     z, c = wide // 2, wide % 2
@@ -116,11 +112,11 @@
 
     def reduce_out(i, part):
         swaps = []
+        planes = (1 - zp, zp)
+        for t in range(2):
+            swap_out[i, t] = part(oc * 2 + planes[t]).astype(BF16)
         for n, (first, last) in enumerate(CHUNKS):
             rows = blocks(first, last)
-            for t in range(2):
-                q = oc * 2 + (zp if t else 1 - zp)
-                swap_out[i, t, rows] = part(q, rows).astype(BF16)
             swap = pltpu.make_async_remote_copy(
                 src_ref=swap_out.at[i, :, rows], dst_ref=swap_in.at[i, :, rows],
                 send_sem=swap_send.at[2 + 3 * i + n], recv_sem=swap_recv.at[2 + 3 * i + n],
@@ -128,12 +124,13 @@
             )
             swap.start()
             swaps.append(swap)
+        for t in range(2):
+            own[t] = part(c * 2 + planes[t])
         for swap, (first, last) in zip(swaps, CHUNKS):
             rows = blocks(first, last)
-            own = [part(c * 2 + (zp if t else 1 - zp), rows) for t in range(2)]
             swap.wait_recv()
             for t in range(2):
-                parts[i, t, rows] = (own[t] + swap_in[i, t, rows].astype(F32)).astype(BF16)
+                parts[i, t, rows] = (own[t, rows] + swap_in[i, t, rows].astype(F32)).astype(BF16)
                 for k in range(first, last):
                     if t and k == PEERS:
                         continue
@@ -156,6 +153,23 @@
         for n in range(PEERS + 1):
             total = total + rows_in[i, 0, n].astype(F32)
         rows_z[i, slot] = total.astype(BF16)
+
+    def send_z(i):
+        piece = rows_z.at[i, z // 2]
+        for d in Z_STEPS:
+            if d % 2 == 0:
+                send(piece, piece, 6 + i, z_sem.at[i], along_z(d))
+        pending.append(lambda: wait(z_others(i), send_sem.at[6 + i]))
+
+    def z_others(i):
+        return rows_z.at[i, pl.ds(0, DEPTH // 2 - 1)]
+
+    def sum_along_z(i):
+        wait(z_others(i), z_sem.at[i])
+        total = rows_z[i, 0].astype(F32)
+        for n in range(1, DEPTH // 2):
+            total = total + rows_z[i, n].astype(F32)
+        return total
 
     for k in range(PEERS):
         there = every.at[c, blocks(BACK[k], BACK[k] + 1)]
@@ -172,34 +186,29 @@
         for k in range(min(last, PEERS) - 1, first - 1, -1):
             wait(every.at[c, blocks(k, k + 1)], block_sem.at[0, k])
         forward(every, 0, first, last)
-        if n == 0:
-            told(0)
-            tell(1)
     enc_load.wait()
     for load in loads:
         load.wait()
     wait(act, load_sem.at[5])
     pre[...] = dot_nn(every[c], enc[half(c), :]) + eb[...]
+    told(0)
+    tell(1)
     forwarded(every, 0)
     both = pre[...] + dot_nn(every[oc], enc[half(oc), :])
     codes[...] = (act[...].astype(F32) * both).astype(BF16)
+
+    reduce_out(0, lambda q: dot_nn(codes[...], dec[:, quarter(q)]))
     told(1)
     tell(2)
-
-    reduce_out(0, lambda q, rows: dot_nn(codes[rows], dec[:, quarter(q)]))
     codes_t[...] = codes[...].T
+    every_t[0] = every[0].T
+    every_t[1] = every[1].T
     told(2)
     pieces_in(0, z // 2)
-    for d in Z_STEPS:
-        if d % 2 == 0:
-            send(rows_z.at[0, z // 2], rows_z.at[0, z // 2], 6, z_sem.at[0], along_z(d))
-    pending.append(lambda: wait(rows_z.at[0, pl.ds(0, DEPTH // 2 - 1)], send_sem.at[6]))
-    every_t[0] = every[0].T
-    every_t[1] = every[1].T
-    wait(rows_z.at[0, pl.ds(0, DEPTH // 2 - 1)], z_sem.at[0])
-    recon = rows_z[0, 0].astype(F32)
-    for n in range(1, DEPTH // 2):
-        recon = recon + rows_z[0, n].astype(F32)
+    send_z(0)
+    dec_t[...] = dec[...].T
+    enc_t[...] = enc[...].T
+    recon = sum_along_z(0)
     recon = recon + db[:, quarter(c * 2 + zp)]
     owned = every[c, mine, quarter(zp)].astype(F32)
     resid[c, zp, mine] = (recon - owned).astype(BF16)
@@ -218,22 +227,21 @@
                 wait(resid.at[c, zp, blocks(k, k + 1)], block_sem.at[2, k])
             wait(resid.at[c, 1 - zp, blocks(k, k + 1)], block_sem.at[1, k])
         forward(resid, 1, first, last)
-    back = dot_nt(resid[c, 0], dec[:, quarter(c * 2)])
-    pre[...] = back + dot_nt(resid[c, 1], dec[:, quarter(c * 2 + 1)])
+    back = dot_nn(resid[c, 0], dec_t[quarter(c * 2), :])
+    pre[...] = back + dot_nn(resid[c, 1], dec_t[quarter(c * 2 + 1), :])
     forwarded(resid, 1)
-    back = pre[...] + dot_nt(resid[oc, 0], dec[:, quarter(oc * 2)])
-    back = back + dot_nt(resid[oc, 1], dec[:, quarter(oc * 2 + 1)])
+    back = pre[...] + dot_nn(resid[oc, 0], dec_t[quarter(oc * 2), :])
+    back = back + dot_nn(resid[oc, 1], dec_t[quarter(oc * 2 + 1), :])
     dpre[...] = (act[...].astype(F32) * back).astype(BF16)
 
-    reduce_out(1, lambda q, rows: dot_nt(dpre[rows], enc[quarter(q), :]))
+    reduce_out(1, lambda q: dot_nn(dpre[...], enc_t[:, quarter(q)]))
     for h in range(2):
         for n in range(2):
             gdec_out[:, quarter(2 * h + n)] = dot_nn(codes_t[...], resid[h, n]).astype(BF16)
         genc_out[half(h), :] = dot_nn(every_t[h], dpre[...]).astype(BF16)
     geb_out[...] = jnp.sum(dpre[...].astype(F32), axis=0, keepdims=True)
-    pieces_in(1, z)
-    for d in Z_STEPS:
-        send(rows_z.at[1, z], rows_z.at[1, z], 7, z_sem.at[1], along_z(d))
+    pieces_in(1, z // 2)
+    send_z(1)
     for q in range(4):
         for k, s in enumerate(subs):
             rows = resid[q // 2, q % 2, blocks(k, k + 1)].astype(F32)
@@ -242,34 +250,26 @@
     for end in pending:
         end()
     pending.clear()
-    everything = rows_z.at[1, pl.ds(0, DEPTH - 1)]
-    wait(everything, z_sem.at[1])
-    for zq in range(2):
-        total = rows_z[1, zq].astype(F32)
-        for n in range(1, DEPTH // 2):
-            total = total + rows_z[1, 2 * n + zq].astype(F32)
-        final[c, zq] = total
-    final_swap = pltpu.make_async_remote_copy(
-        src_ref=final.at[c], dst_ref=final.at[c],
-        send_sem=swap_send.at[8], recv_sem=swap_recv.at[8],
-        device_id=sibling, device_id_type=MESH,
-    )
-    final_swap.start()
-    wait(everything, send_sem.at[7])
-    for zq in range(2):
-        gin_out[:, quarter(c * 2 + zq)] = final[c, zq] - resid[c, zq, mine].astype(F32)
-    final_swap.wait()
-    for zq in range(2):
-        gin_out[:, quarter(oc * 2 + zq)] = final[oc, zq] - resid[oc, zq, mine].astype(F32)
+    q = c * 2 + zp
+    final[q] = sum_along_z(1)
+    mates = [(other_plane, sub), (other_plane + oc - c, sub), sibling]
+    for n, peer in enumerate(mates):
+        pltpu.make_async_remote_copy(
+            src_ref=final.at[q], dst_ref=final.at[q],
+            send_sem=mate_sem.at[0, n], recv_sem=mate_sem.at[1, n],
+            device_id=peer, device_id_type=MESH,
+        ).start()
+    gin_out[:, quarter(q)] = final[q] - resid[c, zp, mine].astype(F32)
+    for n, (h, zq) in ((2, (oc, zp)), (0, (c, 1 - zp)), (1, (oc, 1 - zp))):
+        q = h * 2 + zq
+        wait(final.at[q], mate_sem.at[1, n])
+        gin_out[:, quarter(q)] = final[q] - resid[h, zq, mine].astype(F32)
+    for n in range(3):
+        wait(final.at[0], mate_sem.at[0, n])
 
 
 def place(genc_in, geb_in, gdec_in, gdb_in, gin_in, genc, geb, gdec, gdb, gin, sem):
-    pairs = [(gin_in, gin), (geb_in, geb), (gdb_in, gdb)]
-    for whole_in, whole in ((genc_in, genc), (gdec_in, gdec)):
-        step = whole.shape[0] // 4
-        for n in range(4):
-            rows = pl.ds(n * step, step)
-            pairs.append((whole_in.at[rows], whole.at[rows]))
+    pairs = [(genc_in, genc), (gdec_in, gdec), (gin_in, gin), (geb_in, geb), (gdb_in, gdb)]
     copies = [pltpu.make_async_copy(a, b, sem.at[i]) for i, (a, b) in enumerate(pairs)]
     for copy in copies:
         copy.start()
@@ -298,12 +298,15 @@
         scratch_shapes=[
             pltpu.VMEM((D, LAT), BF16),
             pltpu.VMEM((LAT, D), BF16),
+            pltpu.VMEM((LAT, D), BF16),
+            pltpu.VMEM((D, LAT), BF16),
             pltpu.VMEM((ROWS, LAT), jnp.int32),
             pltpu.VMEM((1, LAT), F32),
             pltpu.VMEM((1, D), F32),
             pltpu.VMEM((2, ROWS, HALF), BF16),
             pltpu.VMEM((2, HALF, ROWS), BF16),
             pltpu.VMEM((ROWS, LAT), F32),
+            pltpu.VMEM((2, ROWS, QUARTER), F32),
             pltpu.VMEM((ROWS, LAT), BF16),
             pltpu.VMEM((LAT, ROWS), BF16),
             pltpu.VMEM((2, 2, ROWS, QUARTER), BF16),
@@ -312,9 +315,9 @@
             pltpu.VMEM((2, 2, ROWS, QUARTER), BF16),
             pltpu.VMEM((2, 2, ROWS, QUARTER), BF16),
             pltpu.VMEM((2, 2, PEERS + 1, OWN, QUARTER), BF16),
-            pltpu.VMEM((2, DEPTH, OWN, QUARTER), BF16),
+            pltpu.VMEM((2, DEPTH // 2, OWN, QUARTER), BF16),
             pltpu.VMEM((PEERS + 1, D), F32),
-            pltpu.VMEM((2, 2, OWN, QUARTER), F32),
+            pltpu.VMEM((4, OWN, QUARTER), F32),
             pltpu.SemaphoreType.DMA((6,)),
             pltpu.SemaphoreType.DMA((9,)),
             pltpu.SemaphoreType.DMA((3, PEERS + 1)),
@@ -322,6 +325,7 @@
             pltpu.SemaphoreType.DMA((2,)),
             pltpu.SemaphoreType.DMA((9,)),
             pltpu.SemaphoreType.DMA((9,)),
+            pltpu.SemaphoreType.DMA((2, 3)),
             pltpu.SemaphoreType.REGULAR((3,)),
         ],
         compiler_params=pltpu.CompilerParams(
@@ -337,7 +341,7 @@
         out_shape=shapes,
         in_specs=[vmem] * 5,
         out_specs=[anywhere] * 5,
-        scratch_shapes=[pltpu.SemaphoreType.DMA((11,))],
+        scratch_shapes=[pltpu.SemaphoreType.DMA((5,))],
         compiler_params=pltpu.CompilerParams(vmem_limit_bytes=2**18),
         name="place",
     )(*(pltpu.with_memory_space_constraint(a, pltpu.VMEM) for a in results))

time: 63.8 us -> 62.1 us (0.973)
  Pallas kernels: 63 us -> 61.2 us
    pallas_call x1, Pallas kernels: 61.6 us -> 59.9 us  [per_device(): pl.pallas_call(kernel, out_shape=[pltpu.VMEM(s.shape, s.dtype) for s in s...]
where the time goes in v5:
time: 62.1 us; the launch traced here: 61.9 us
  Pallas kernels  61.2 us (99%)
  between operations  0.64 us (1%)
    pallas_call x1, Pallas kernels, per_device(): pl.pallas_call(kernel, out_shape=[pltpu.VMEM(s.shape, s.dtype) for s in s...  59.9 us
    pallas_call x1, Pallas kernels, per_device(): pl.pallas_call(place, out_shape=shapes, in_specs=[vmem] * 5, out_specs=[a...  1.37 us

profile of v5, /device:TPU:1, one launch (start us, length us, event | category | flops | bytes accessed | tf_op | source)
XLA Modules:
  0.0 61.9 jit_solution(11482710055001072801)
XLA Ops:
  0.6 59.9 %sae_backward.1 = (bf16[1024,512]{1,0:T(8,128)(2,1)S(1)}, f32[1,512]{1,0:T(1,128)S(1)}, bf16[512,1024]{1,0:T(8,128)(2,1)S(1)}, f32[1,1024]{1,0:T(1,128)S(1)}, f32[16,1024]{1,0:T(8,128)S(1)}) custom-call(bf16[16,1024]{1,0:T(8,128)(2,1)} %pas_in.1, bf16[1024,512]{1,0:T(8,128)(2,1)} %enc_in.1, f32[1,512]{1,0:T(1,128)} %bitcast.6, bf16[512,1024]{1,0:T(8,128)(2,1)} %dec_in.1, ...), custom_call_target="tpu_custom_call" | custom-call | flops 1342177280 | bytes 5242880 | tf_op jit(solution)/shard_map/sae_backward/pallas_call | solution.py:293
  60.5 1.4 %place.1 = (bf16[1024,512]{1,0:T(8,128)(2,1)}, f32[1,512]{1,0:T(1,128)}, bf16[512,1024]{1,0:T(8,128)(2,1)}, f32[1,1024]{1,0:T(1,128)}, f32[16,1024]{1,0:T(8,128)}) custom-call(bf16[1024,512]{1,0:T(8,128)(2,1)S(1)} %get-tuple-element.15.genc_in, f32[1,512]{1,0:T(1,128)S(1)} %get-tuple-element.16.geb_in, bf16[512,1024]{1,0:T(8,128)(2,1)S(1)} %get-tuple-element.17.gdec_in, ...), custom_call_target="tpu_custom_call" | custom-call | tf_op jit(solution)/shard_map/place/pallas_call | solution.py:339

commit v6 on v5

--- a/solution.py
+++ b/solution.py
@@ -24,7 +24,6 @@
 BACK = [OFFSETS.index((-dx % SIDE, -dy % SIDE)) for dx, dy in OFFSETS]
 PEERS = len(OFFSETS) - 1
 FORWARD = ((11, 16), (8, 11), (5, 8), (3, 5), (1, 3), (0, 1))
-CHUNKS = ((0, 5), (5, 11), (11, 16))
 Z_STEPS = sorted(range(1, DEPTH), key=lambda d: -ring(d, DEPTH))
 
 
@@ -115,29 +114,25 @@
         planes = (1 - zp, zp)
         for t in range(2):
             swap_out[i, t] = part(oc * 2 + planes[t]).astype(BF16)
-        for n, (first, last) in enumerate(CHUNKS):
-            rows = blocks(first, last)
             swap = pltpu.make_async_remote_copy(
-                src_ref=swap_out.at[i, :, rows], dst_ref=swap_in.at[i, :, rows],
-                send_sem=swap_send.at[2 + 3 * i + n], recv_sem=swap_recv.at[2 + 3 * i + n],
+                src_ref=swap_out.at[i, t], dst_ref=swap_in.at[i, t],
+                send_sem=swap_send.at[2 + 3 * i + t], recv_sem=swap_recv.at[2 + 3 * i + t],
                 device_id=sibling, device_id_type=MESH,
             )
             swap.start()
             swaps.append(swap)
         for t in range(2):
             own[t] = part(c * 2 + planes[t])
-        for swap, (first, last) in zip(swaps, CHUNKS):
-            rows = blocks(first, last)
+        for t, swap in enumerate(swaps):
             swap.wait_recv()
-            for t in range(2):
-                parts[i, t, rows] = (own[t, rows] + swap_in[i, t, rows].astype(F32)).astype(BF16)
-                for k in range(first, last):
-                    if t and k == PEERS:
-                        continue
-                    send(
-                        parts.at[i, t, blocks(k, k + 1)], rows_in.at[i, t, BACK[k]],
-                        2 + 2 * i + t, piece_sem.at[i, t], (wide if t else other_plane, subs[k]),
-                    )
+            parts[i, t] = (own[t] + swap_in[i, t].astype(F32)).astype(BF16)
+            for k in range(PEERS + 1):
+                if t and k == PEERS:
+                    continue
+                send(
+                    parts.at[i, t, blocks(k, k + 1)], rows_in.at[i, t, BACK[k]],
+                    2 + 2 * i + t, piece_sem.at[i, t], (wide if t else other_plane, subs[k]),
+                )
             pending.append(swap.wait_send)
         rows_in[i, 1, PEERS] = parts[i, 1, mine]
 

time: 62.1 us -> 62.8 us (1.011)
  Pallas kernels: 61.2 us -> 62 us
    pallas_call x1, Pallas kernels: 59.9 us -> 60.6 us  [per_device(): pl.pallas_call(kernel, out_shape=[pltpu.VMEM(s.shape, s.dtype) for s in s...]
where the time goes in v6:
time: 62.8 us; the launch traced here: 62.7 us
  Pallas kernels  62 us (99%)
  between operations  0.64 us (1%)
    pallas_call x1, Pallas kernels, per_device(): pl.pallas_call(kernel, out_shape=[pltpu.VMEM(s.shape, s.dtype) for s in s...  60.6 us
    pallas_call x1, Pallas kernels, per_device(): pl.pallas_call(place, out_shape=shapes, in_specs=[vmem] * 5, out_specs=[a...  1.37 us

profile of v6, /device:TPU:1, one launch (start us, length us, event | category | flops | bytes accessed | tf_op | source)
XLA Modules:
  0.0 62.7 jit_solution(7038843831387548233)
XLA Ops:
  0.6 60.6 %sae_backward.1 = (bf16[1024,512]{1,0:T(8,128)(2,1)S(1)}, f32[1,512]{1,0:T(1,128)S(1)}, bf16[512,1024]{1,0:T(8,128)(2,1)S(1)}, f32[1,1024]{1,0:T(1,128)S(1)}, f32[16,1024]{1,0:T(8,128)S(1)}) custom-call(bf16[16,1024]{1,0:T(8,128)(2,1)} %pas_in.1, bf16[1024,512]{1,0:T(8,128)(2,1)} %enc_in.1, f32[1,512]{1,0:T(1,128)} %bitcast.6, bf16[512,1024]{1,0:T(8,128)(2,1)} %dec_in.1, ...), custom_call_target="tpu_custom_call" | custom-call | flops 1342177280 | bytes 5242880 | tf_op jit(solution)/shard_map/sae_backward/pallas_call | solution.py:288
  61.3 1.4 %place.1 = (bf16[1024,512]{1,0:T(8,128)(2,1)}, f32[1,512]{1,0:T(1,128)}, bf16[512,1024]{1,0:T(8,128)(2,1)}, f32[1,1024]{1,0:T(1,128)}, f32[16,1024]{1,0:T(8,128)}) custom-call(bf16[1024,512]{1,0:T(8,128)(2,1)S(1)} %get-tuple-element.15.genc_in, f32[1,512]{1,0:T(1,128)S(1)} %get-tuple-element.16.geb_in, bf16[512,1024]{1,0:T(8,128)(2,1)S(1)} %get-tuple-element.17.gdec_in, ...), custom_call_target="tpu_custom_call" | custom-call | tf_op jit(solution)/shard_map/place/pallas_call | solution.py:334
